TPU v7x, 128 devices: a whole 4x4x4 slice. The times are simulated.
128 devices in a mesh: role: 2 (over core), dev: 64 (over z, x, y).
Axes of the slice: x: 4, y: 4, z: 4, core: 2. Of those that a mesh axis runs over, the one named last changes fastest.
Arguments:
- queries: bfloat16 [4096, 8192], P(('role', 'dev')), may hold values from -192 to 192, as said below
- key_value_cache: bfloat16 [1024, 256, 1024], P(('role', 'dev')), may hold values from -6 to 6
- guessed_key_value: bfloat16 [4096, 1024], P(('role', 'dev')), may hold values from -6 to 6
- cache_length_per_request: int32 [1024], P(('role', 'dev')), may hold values from 1 to 256, 131072 in all
- moe_rows: bfloat16 [4096, 4096], P(('role', 'dev')), may hold values from -6 to 6
- expert_ids: int32 [4096, 8], P(('role', 'dev')), may hold values from 0 to 127, all different within a row; in each aligned block of 16 rows (0 to 15, 16 to 31, ...) at most 2 rows name the same one
- gate_weights: float32 [4096, 8], P(('role', 'dev')), may hold values from 0.05 to 1
- expert_in: bfloat16 [128, 4096, 1536], P(('role', 'dev')), may hold values from -0.09375 to 0.09375
- expert_down: bfloat16 [128, 768, 4096], P(('role', 'dev')), may hold values from -0.21875 to 0.21875
Outputs:
- attended: bfloat16 [4096, 8192], P(('role', 'dev'))
- moe_out: bfloat16 [4096, 4096], P(('role', 'dev'))
Inputs may be any that keep to these rules, and one draw needn't show every extreme that they name: queries of the shown draw lie within -12 and 12. Some request's cache_length_per_request is exactly 256. `expert_ids`: each row names 8 different experts; within each aligned block of 16 rows no expert is named by more than 2 rows, and in every draw some block names some expert exactly 2 times.
All inputs are finite; a program needn't handle non-finite values. No bound on the sum of `cache_length_per_request` on one device may be relied on, other than what follows from the above.
Results may differ from a plain program's by a relative error of at most 0.0058.
Values may be sent and summed in bfloat16 or wider, within the bound.
No kernel may reach another device: no remote copies, remote signals or barrier semaphores. Data moves between devices by JAX's collectives and lax.ppermute only.
A program may use at most 128 MiB of HBM per device.

v0:
```python
import jax
import jax.numpy as jnp
from jax import lax
from jax.sharding import PartitionSpec as P

QUERY_HEADS = 64
KEY_VALUE_HEADS = 4
HEAD_SIZE = 128


def attend(queries, key_value_cache, guessed_key_value, cache_length_per_request):
    request_number, slot_positions, joint_width = key_value_cache.shape
    feature_width = joint_width // 2
    guessed_count = queries.shape[0] // request_number
    query_group_size = QUERY_HEADS // KEY_VALUE_HEADS
    scale = float(HEAD_SIZE) ** (-0.5)
    query_rows = queries.reshape(
        request_number, guessed_count, KEY_VALUE_HEADS, query_group_size, HEAD_SIZE
    )
    cache_key_rows = key_value_cache[:, :, :feature_width].reshape(
        request_number, slot_positions, KEY_VALUE_HEADS, HEAD_SIZE
    )
    cache_value_rows = key_value_cache[:, :, feature_width:].reshape(
        request_number, slot_positions, KEY_VALUE_HEADS, HEAD_SIZE
    )
    guessed_rows = guessed_key_value.reshape(request_number, guessed_count, joint_width)
    guessed_keys = guessed_rows[:, :, :feature_width].reshape(
        request_number, guessed_count, KEY_VALUE_HEADS, HEAD_SIZE
    )
    guessed_values = guessed_rows[:, :, feature_width:].reshape(
        request_number, guessed_count, KEY_VALUE_HEADS, HEAD_SIZE
    )
    scores_cache = (
        jnp.einsum(
            "rsngd,rcnd->rsngc", query_rows, cache_key_rows, preferred_element_type=jnp.float32
        )
        * scale
    )
    scores_fresh = (
        jnp.einsum(
            "rsngd,rjnd->rsngj", query_rows, guessed_keys, preferred_element_type=jnp.float32
        )
        * scale
    )
    valid_cache = (jnp.arange(slot_positions)[None, :] < cache_length_per_request[:, None])[
        :, None, None, None, :
    ]
    valid_fresh = (jnp.arange(guessed_count)[None, :] <= jnp.arange(guessed_count)[:, None])[
        None, :, None, None, :
    ]
    scores_cache = jnp.where(valid_cache, scores_cache, -jnp.inf)
    scores_fresh = jnp.where(valid_fresh, scores_fresh, -jnp.inf)
    highest = jnp.maximum(
        jnp.max(scores_cache, axis=-1, keepdims=True), jnp.max(scores_fresh, axis=-1, keepdims=True)
    )
    exp_cache = jnp.exp(scores_cache - highest)
    exp_fresh = jnp.exp(scores_fresh - highest)
    total = jnp.sum(exp_cache, axis=-1, keepdims=True) + jnp.sum(exp_fresh, axis=-1, keepdims=True)
    probs_cache = (exp_cache / total).astype(jnp.bfloat16)
    probs_fresh = (exp_fresh / total).astype(jnp.bfloat16)
    output = jnp.einsum(
        "rsngc,rcnd->rsngd", probs_cache, cache_value_rows, preferred_element_type=jnp.float32
    )
    output = output + jnp.einsum(
        "rsngj,rjnd->rsngd", probs_fresh, guessed_values, preferred_element_type=jnp.float32
    )
    return output.reshape(request_number * guessed_count, QUERY_HEADS * HEAD_SIZE).astype(
        jnp.bfloat16
    )


def body(
    queries,
    key_value_cache,
    guessed_key_value,
    cache_length_per_request,
    moe_rows,
    expert_ids,
    gate_weights,
    expert_in,
    expert_down,
):
    expert_count = lax.axis_size(("role", "dev"))
    row_count, top_count = expert_ids.shape
    model_width = moe_rows.shape[1]
    hidden_width = expert_down.shape[1]
    half_count = row_count // 2
    half_slots = max(2, row_count * top_count // expert_count)
    slot_count = 2 * half_slots
    attended = attend(queries, key_value_cache, guessed_key_value, cache_length_per_request)
    chosen = (
        expert_ids[:, :, None] == jnp.arange(expert_count, dtype=jnp.int32)[None, None, :]
    ).astype(jnp.int32)
    member = jnp.sum(chosen, axis=1)
    halves_view = member.reshape(2, half_count, expert_count)
    ranks = (jnp.cumsum(halves_view, axis=1) - halves_view).reshape(row_count, expert_count)
    half_index = (jnp.arange(row_count, dtype=jnp.int32) // half_count)[:, None]
    slot = half_index * half_slots + ranks
    placing = (slot.T[:, None, :] == jnp.arange(slot_count, dtype=jnp.int32)[None, :, None]) & (
        member.T[:, None, :] > 0
    )
    outgoing = jnp.einsum(
        "est,td->esd", placing.astype(jnp.bfloat16), moe_rows, preferred_element_type=jnp.float32
    ).astype(jnp.bfloat16)
    block_in = lax.all_to_all(outgoing, ("role", "dev"), split_axis=0, concat_axis=0, tiled=True)
    rows = block_in.reshape(-1, model_width)
    joint = jnp.dot(rows, expert_in[0], preferred_element_type=jnp.float32)
    hidden = (jax.nn.silu(joint[:, :hidden_width]) * joint[:, hidden_width:]).astype(jnp.bfloat16)
    result = jnp.dot(hidden, expert_down[0], preferred_element_type=jnp.float32).astype(
        jnp.bfloat16
    )
    results = result.reshape(block_in.shape)
    returned = lax.all_to_all(results, ("role", "dev"), split_axis=0, concat_axis=0, tiled=True)
    route_weights = gate_weights / jnp.sum(gate_weights, axis=-1, keepdims=True)
    slot_taken = jnp.take_along_axis(slot, expert_ids, axis=1)
    flat_index = expert_ids * slot_count + slot_taken
    picked = returned.reshape(-1, model_width)[flat_index]
    mixed = jnp.sum(route_weights[:, :, None] * picked.astype(jnp.float32), axis=1)
    return (attended, mixed.astype(jnp.bfloat16))


def solution(mesh):
    return jax.shard_map(
        body,
        mesh=mesh,
        in_specs=(
            P(("role", "dev"), None),
            P(("role", "dev"), None, None),
            P(("role", "dev"), None),
            P(("role", "dev")),
            P(("role", "dev"), None),
            P(("role", "dev"), None),
            P(("role", "dev"), None),
            P(("role", "dev"), None, None),
            P(("role", "dev"), None, None),
        ),
        out_specs=(P(("role", "dev"), None), P(("role", "dev"), None)),
        check_vma=False,
    )
```

profile of v0, /device:TPU:1, one launch (start us, length us, event | category | flops | bytes accessed | tf_op | source)
XLA Modules:
  0.0 179.5 jit_solution(17069054378423689428)
XLA Ops:
  0.7 0.8 copy.51
  1.5 0.1 convert_reduce_fusion
  1.6 0.1 fusion.30
  1.7 1.3 convolution_convert_fusion
  3.0 3.2 %copy.52 = bf16[128,4,4096]{2,1,0:T(4,128)(2,1)S(1)} copy(bf16[128,4,4096]{2,0,1:T(8,128)(2,1)S(1)} %convolution_convert_fusion) | data formatting | bytes 8388608 | tf_op jit(solution)/shard_map/convert_element_type | solution.py:104
  6.3 64.5 %all_to_all.10 = bf16[128,4,4096]{2,1,0:T(4,128)(2,1)} all-to-all(bf16[128,4,4096]{2,1,0:T(4,128)(2,1)S(1)} %copy.52), channel_id=1, replica_groups=mesh['role'=2,'dev'=64] {'role','dev'}, dimensions={0} | all-to-all | bytes 8388608 | tf_op jit(solution)/shard_map/all_to_all | solution.py:105
  70.8 6.9 %reshape.116 = bf16[512,4096]{1,0:T(8,128)(2,1)} reshape(bf16[128,4,4096]{2,1,0:T(4,128)(2,1)} %all_to_all.10) | data formatting | bytes 8388608 | tf_op jit(solution)/shard_map/reshape | solution.py:106
  77.7 10.5 %fusion = f32[512,1536]{1,0:T(8,128)S(1)} fusion(bf16[512,4096]{1,0:T(8,128)(2,1)} %reshape.116, bf16[1,4096,1536]{2,1,0:T(8,128)(2,1)} %param.16), kind=kOutput, calls=%fused_computation.2 | convolution fusion | flops 6442450944 | bytes 19922944 | tf_op jit(solution)/shard_map/dot_general | solution.py:107
  88.2 7.8 %fusion.4 = bf16[512,4096]{1,0:T(8,128)(2,1)} fusion(bf16[1,768,4096]{2,1,0:T(8,128)(2,1)} %param.17, f32[512,1536]{1,0:T(8,128)S(1)} %fusion), kind=kOutput, calls=%fused_computation.6 | convolution fusion | flops 3225681920 | bytes 13631488 | tf_op jit(solution)/shard_map/dot_general | solution.py:109
  96.0 7.2 %reshape.117 = bf16[128,4,4096]{2,1,0:T(4,128)(2,1)} reshape(bf16[512,4096]{1,0:T(8,128)(2,1)} %fusion.4) | data formatting | bytes 8388608 | tf_op jit(solution)/shard_map/reshape | solution.py:112
  103.2 7.6 %all-to-all-start.1 = ((bf16[128,4,4096]{2,1,0:T(4,128)(2,1)}), bf16[128,4,4096]{2,1,0:T(4,128)(2,1)}, u32[]{:S(2)}, u32[]{:S(2)}) async-start(bf16[128,4,4096]{2,1,0:T(4,128)(2,1)} %reshape.117), calls=%async_computation.1 | async-start | bytes 8388608 | tf_op jit(solution)/shard_map/all_to_all | solution.py:113
  110.8 4.6 %fusion.35 = (bf16[8,256,512]{2,1,0:T(8,128)(2,1)}, bf16[8,256,512]{2,1,0:T(8,128)(2,1)}) fusion(bf16[8,256,1024]{2,1,0:T(8,128)(2,1)} %param.10), kind=kLoop, calls=%fused_computation.62 | loop fusion | bytes 8388608 | tf_op jit(solution)/shard_map/slice | solution.py:20
  115.4 2.9 %copy.65 = bf16[8,256,512]{1,2,0:T(8,128)(2,1)S(1)} copy(bf16[8,256,512]{2,1,0:T(8,128)(2,1)} %get-tuple-element.2) | data formatting | bytes 4194304
  118.4 0.1 copy.67
  118.6 3.9 %copy.66 = bf16[8,256,512]{1,2,0:T(8,128)(2,1)} copy(bf16[8,256,512]{2,1,0:T(8,128)(2,1)} %get-tuple-element.3) | data formatting | bytes 4194304
  122.6 1.4 fusion.36
  124.0 0.6 bitcast_reduce_fusion
  124.6 0.3 fusion.23
  124.8 0.9 fusion.9
  125.8 0.4 copy-done.2
  126.1 1.3 fusion.15
  127.5 0.4 fusion.12
  127.9 1.0 convert_element_type.38
  129.0 0.1 reshape.128
  129.1 1.9 %gather_fusion.1 = s32[256]{0:T(256)S(1)} fusion(s32[32,128]{1,0:T(8,128)S(1)} %fusion.30, s32[256]{0:T(256)S(1)} %reshape.128), kind=kCustom, calls=%fused_computation.1 | custom fusion | bytes 4096 | tf_op jit(solution)/shard_map/jit(take_along_axis)/gather | solution.py:115
  131.0 0.1 reshape.131
  131.1 0.1 reshape.122
  131.2 0.1 copy.50
  131.3 32.3 %all-to-all-done.1 = bf16[128,4,4096]{2,1,0:T(4,128)(2,1)} async-done(((bf16[128,4,4096]{2,1,0:T(4,128)(2,1)}), bf16[128,4,4096]{2,1,0:T(4,128)(2,1)}, u32[]{:S(2)}, u32[]{:S(2)}) %all-to-all-start.1) | async-done | bytes 4194336 | tf_op jit(solution)/shard_map/all_to_all | solution.py:113
  163.6 6.9 %reshape.118 = bf16[512,4096]{1,0:T(8,128)(2,1)} reshape(bf16[128,4,4096]{2,1,0:T(4,128)(2,1)} %all-to-all-done.1) | data formatting | bytes 8388608 | tf_op jit(solution)/shard_map/reshape | solution.py:117
  170.5 6.7 %gather_fusion = bf16[256,4096]{1,0:T(8,128)(2,1)S(1)} fusion(bf16[512,4096]{1,0:T(8,128)(2,1)} %reshape.118, s32[1024]{0:T(1024)S(1)} %pad_clamp_fusion), kind=kCustom, calls=%fused_computation | custom fusion | bytes 4195328 | tf_op jit(solution)/shard_map/gather | solution.py:117
  177.1 2.3 %fusion.7 = bf16[32,4096]{1,0:T(8,128)(2,1)} fusion(bf16[256,4096]{1,0:T(8,128)(2,1)S(1)} %gather_fusion, f32[32,8]{1,0:T(8,128)S(1)} %copy.50), kind=kLoop, calls=%fused_computation.9 | loop fusion | flops 3014656 | bytes 2360320 | tf_op jit(solution)/shard_map/reduce_sum | solution.py:118
  (27 shorter events, 0.3 us)
Async XLA Ops:
  0.6 1.1 copy-start
  103.2 60.3 %all-to-all-start.1 = ((bf16[128,4,4096]{2,1,0:T(4,128)(2,1)}), bf16[128,4,4096]{2,1,0:T(4,128)(2,1)}, u32[]{:S(2)}, u32[]{:S(2)}) async-start(bf16[128,4,4096]{2,1,0:T(4,128)(2,1)} %reshape.117), calls=%async_computation.1 | async-start | bytes 8388608 | tf_op jit(solution)/shard_map/all_to_all | solution.py:113
  115.4 2.9 %copy-start.3 = (bf16[32,8192]{1,0:T(8,128)(2,1)S(1)}, bf16[32,8192]{1,0:T(8,128)(2,1)}, u32[]{:S(2)}) copy-start(bf16[32,8192]{1,0:T(8,128)(2,1)} %param.9) | copy-start | bytes 1572868
  115.4 3.1 %copy-start.4 = (bf16[32,1024]{1,0:T(8,128)(2,1)S(1)}, bf16[32,1024]{1,0:T(8,128)(2,1)}, u32[]{:S(2)}) copy-start(bf16[32,1024]{1,0:T(8,128)(2,1)} %param.11) | copy-start | bytes 196612
  118.5 3.9 %copy-start.6 = (s32[8]{0:T(128)S(1)}, s32[8]{0:T(128)}, u32[]{:S(2)}) copy-start(s32[8]{0:T(128)} %param.12) | copy-start | bytes 100
  124.5 1.6 copy-start.2
  129.1 2.1 %copy-start.5 = (f32[32,8]{0,1:T(8,128)S(1)}, f32[32,8]{0,1:T(8,128)}, u32[]{:S(2)}) copy-start(f32[32,8]{0,1:T(8,128)} %param.15) | copy-start | bytes 3076
  170.5 9.0 %copy-start.1 = (bf16[32,4096]{1,0:T(8,128)(2,1)S(1)}, bf16[32,4096]{1,0:T(8,128)(2,1)}, u32[]{:S(2)}) copy-start(bf16[32,4096]{1,0:T(8,128)(2,1)} %param.13) | copy-start | bytes 786436
where the time goes:
time: 181 us; the launch traced here: 179 us
  blocking collectives  64.5 us (36%)
  local copies, waits for them, and re-layouts  47 us (26%)
  waiting for transfers between devices  32.3 us (18%)
  matrix products  23.3 us (13%)
  starting transfers between devices  7.57 us (4%)
  other arithmetic  3.91 us (2%)
    all_to_all x1, blocking collectives, body(): lax.all_to_all(outgoing, ('role', 'dev'), split_axis=0, concat_axis=0, ti...  64.5 us
    all_to_all x1, waiting for transfers between devices, body(): lax.all_to_all(results, ('role', 'dev'), split_axis=0, concat_axis=0, til...  32.3 us
    dot_general x1, matrix products, body(): joint = jnp.dot(rows, expert_in[0], preferred_element_type=jnp.float32)  10.5 us
    unnamed x18, local copies, waits for them, and re-layouts  8.16 us
    dot_general x1, matrix products, body(): jnp.dot(hidden, expert_down[0], preferred_element_type=jnp.float32)  7.83 us
    all_to_all x1, starting transfers between devices, body(): lax.all_to_all(results, ('role', 'dev'), split_axis=0, concat_axis=0, til...  7.57 us
    reshape x1, local copies, waits for them, and re-layouts, body(): results = result.reshape(block_in.shape)  7.19 us
    reshape x1, local copies, waits for them, and re-layouts, body(): picked = returned.reshape(-1, model_width)[flat_index]  6.91 us
  transfers between devices with their start and end apart: 1, of which 1 were waited for; matrix products, arithmetic and copies ran while one was open for 11% of the time, Pallas kernels for 0%

commit v1 on v0

--- a/solution.py
+++ b/solution.py
@@ -1,11 +1,17 @@
+import functools
+
 import jax
 import jax.numpy as jnp
 from jax import lax
+from jax.experimental import pallas as pl
+from jax.experimental.pallas import tpu as pltpu
 from jax.sharding import PartitionSpec as P
 
 QUERY_HEADS = 64
 KEY_VALUE_HEADS = 4
 HEAD_SIZE = 128
+BLOCK_ROWS = 16
+BLOCK_SLOTS = 2
 
 
 def attend(queries, key_value_cache, guessed_key_value, cache_length_per_request):
@@ -66,6 +72,186 @@
     )
     return output.reshape(request_number * guessed_count, QUERY_HEADS * HEAD_SIZE).astype(
         jnp.bfloat16
+    )
+
+
+def expert_spots(ids, base, chips):
+    token_count, top_count = ids.shape
+    slots = token_count // BLOCK_ROWS * BLOCK_SLOTS
+    shape = (token_count, chips * slots)
+    column = lax.broadcasted_iota(jnp.int32, shape, 1)
+    expert = base + column // slots
+    matches = [ids[:, k : k + 1] == expert for k in range(top_count)]
+    member = functools.reduce(jnp.logical_or, matches)
+    here = lax.broadcasted_iota(jnp.int32, (token_count, token_count), 0)
+    there = lax.broadcasted_iota(jnp.int32, (token_count, token_count), 1)
+    earlier = (there < here) & (there // BLOCK_ROWS == here // BLOCK_ROWS)
+    ranks = jnp.dot(
+        jnp.where(earlier, 1.0, 0.0).astype(jnp.bfloat16),
+        jnp.where(member, 1.0, 0.0).astype(jnp.bfloat16),
+        preferred_element_type=jnp.float32,
+    ).astype(jnp.int32)
+    block = lax.broadcasted_iota(jnp.int32, shape, 0) // BLOCK_ROWS
+    taken = member & (block * BLOCK_SLOTS + ranks == column % slots)
+    return matches, taken
+
+
+def place_kernel(chips, base_ref, own_ids, other_ids, own_ref, other_ref, out_ref, spots):
+    @pl.when(pl.program_id(0) == 0)
+    def _():
+        ids = jnp.concatenate([own_ids[...], other_ids[...]], axis=0)
+        _, taken = expert_spots(ids, base_ref[0], chips)
+        spots[...] = jnp.where(taken, 1.0, 0.0).astype(jnp.bfloat16)
+
+    rows = jnp.concatenate([own_ref[...], other_ref[...]], axis=0)
+    out_ref[...] = lax.dot_general(
+        spots[...], rows, (((0,), (0,)), ((), ())), preferred_element_type=jnp.float32
+    ).astype(jnp.bfloat16)
+
+
+def place(base, own_ids, other_ids, own, other, chips):
+    row_count, width = own.shape
+    slots = 2 * row_count // BLOCK_ROWS * BLOCK_SLOTS
+    tile = min(width, 1024)
+    whole = pl.BlockSpec(own_ids.shape, lambda i: (0, 0))
+    part = pl.BlockSpec((row_count, tile), lambda i: (0, i))
+    return pl.pallas_call(
+        functools.partial(place_kernel, chips),
+        grid=(width // tile,),
+        out_shape=pltpu.HBM((chips * slots, width), jnp.bfloat16),
+        in_specs=[pl.BlockSpec(memory_space=pltpu.SMEM), whole, whole, part, part],
+        out_specs=pl.BlockSpec((chips * slots, tile), lambda i: (0, i)),
+        scratch_shapes=[pltpu.VMEM((2 * row_count, chips * slots), jnp.bfloat16)],
+        compiler_params=pltpu.CompilerParams(vmem_limit_bytes=16 << 20),
+        name="place_rows",
+    )(base, own_ids, other_ids, own, other)
+
+
+def mix_kernel(
+    chips, base_ref, own_ids, other_ids, own_gates, other_gates, in_ref, own_ref, other_ref, spread
+):
+    row_count = own_ids.shape[0]
+    token_count = 2 * row_count
+
+    @pl.when(pl.program_id(0) == 0)
+    def _():
+        ids = jnp.concatenate([own_ids[...], other_ids[...]], axis=0)
+        gates = jnp.concatenate([own_gates[...], other_gates[...]], axis=0)
+        matches, taken = expert_spots(ids, base_ref[0], chips)
+        route = gates / jnp.sum(gates, axis=-1, keepdims=True)
+        weight = sum(
+            jnp.where(match, route[:, k : k + 1], 0.0) for k, match in enumerate(matches)
+        )
+        weight = jnp.where(taken, weight, 0.0)
+        high = weight.astype(jnp.bfloat16)
+        spread[:token_count] = high
+        spread[token_count:] = (weight - high.astype(jnp.float32)).astype(jnp.bfloat16)
+
+    total = jnp.dot(spread[...], in_ref[...], preferred_element_type=jnp.float32)
+    total = total[:token_count] + total[token_count:]
+    own_ref[...] = total[:row_count]
+    other_ref[...] = total[row_count:].astype(jnp.bfloat16)
+
+
+def mix(base, own_ids, other_ids, own_gates, other_gates, returned, chips):
+    row_count = own_ids.shape[0]
+    slot_total, width = returned.shape
+    tile = min(width, 1024)
+    whole = pl.BlockSpec(own_ids.shape, lambda i: (0, 0))
+    part = pl.BlockSpec((row_count, tile), lambda i: (0, i))
+    return pl.pallas_call(
+        functools.partial(mix_kernel, chips),
+        grid=(width // tile,),
+        out_shape=(
+            jax.ShapeDtypeStruct((row_count, width), jnp.float32),
+            jax.ShapeDtypeStruct((row_count, width), jnp.bfloat16),
+        ),
+        in_specs=[
+            pl.BlockSpec(memory_space=pltpu.SMEM),
+            whole,
+            whole,
+            whole,
+            whole,
+            pl.BlockSpec((slot_total, tile), lambda i: (0, i)),
+        ],
+        out_specs=(part, part),
+        scratch_shapes=[pltpu.VMEM((4 * row_count, slot_total), jnp.bfloat16)],
+        compiler_params=pltpu.CompilerParams(vmem_limit_bytes=16 << 20),
+        name="mix_results",
+    )(base, own_ids, other_ids, own_gates, other_gates, returned)
+
+
+def expert_kernel(rows_hbm, in_ref, down_ref, out_hbm, rows, joint, hidden, out, row_sems, out_sems):
+    in_steps, _, depth = rows.shape
+    out_steps, _, width = out.shape
+    hidden_width = hidden.shape[1]
+
+    def arrive(step):
+        return pltpu.make_async_copy(
+            rows_hbm.at[:, pl.ds(step * depth, depth)], rows.at[step], row_sems.at[step]
+        )
+
+    def leave(step):
+        return pltpu.make_async_copy(
+            out.at[step], out_hbm.at[:, pl.ds(step * width, width)], out_sems.at[step]
+        )
+
+    for step in range(in_steps):
+        arrive(step).start()
+    for step in range(in_steps):
+        arrive(step).wait()
+        part = jnp.dot(
+            rows[step],
+            in_ref[0, step * depth : (step + 1) * depth, :],
+            preferred_element_type=jnp.float32,
+        )
+        joint[...] = part if step == 0 else joint[...] + part
+    gate = joint[:, :hidden_width]
+    hidden[...] = (gate / (1.0 + jnp.exp(-gate)) * joint[:, hidden_width:]).astype(jnp.bfloat16)
+    for step in range(out_steps):
+        out[step] = jnp.dot(
+            hidden[...],
+            down_ref[0, :, step * width : (step + 1) * width],
+            preferred_element_type=jnp.float32,
+        ).astype(jnp.bfloat16)
+        leave(step).start()
+    for step in range(out_steps):
+        leave(step).wait()
+
+
+def expert(rows, expert_in, expert_down):
+    row_count, width = rows.shape
+    hidden_width = expert_down.shape[1]
+    depth = min(width, 1024)
+    steps = width // depth
+    return pl.pallas_call(
+        expert_kernel,
+        out_shape=pltpu.HBM((row_count, width), jnp.bfloat16),
+        in_specs=[
+            pl.BlockSpec(memory_space=pl.ANY),
+            pl.BlockSpec(memory_space=pltpu.VMEM),
+            pl.BlockSpec(memory_space=pltpu.VMEM),
+        ],
+        out_specs=pl.BlockSpec(memory_space=pl.ANY),
+        scratch_shapes=[
+            pltpu.VMEM((steps, row_count, depth), jnp.bfloat16),
+            pltpu.VMEM((row_count, 2 * hidden_width), jnp.float32),
+            pltpu.VMEM((row_count, hidden_width), jnp.bfloat16),
+            pltpu.VMEM((steps, row_count, depth), jnp.bfloat16),
+            pltpu.SemaphoreType.DMA((steps,)),
+            pltpu.SemaphoreType.DMA((steps,)),
+        ],
+        compiler_params=pltpu.CompilerParams(vmem_limit_bytes=20 << 20),
+        cost_estimate=pl.CostEstimate(
+            flops=6 * row_count * width * hidden_width,
+            bytes_accessed=4 * row_count * width,
+            transcendentals=row_count * hidden_width,
+        ),
+        name="expert_layer",
+    )(
+        pltpu.with_memory_space_constraint(rows, pltpu.HBM),
+        pltpu.with_memory_space_constraint(expert_in, pltpu.VMEM),
+        pltpu.with_memory_space_constraint(expert_down, pltpu.VMEM),
     )
 
 
@@ -80,43 +266,34 @@
     expert_in,
     expert_down,
 ):
-    expert_count = lax.axis_size(("role", "dev"))
-    row_count, top_count = expert_ids.shape
+    role = lax.axis_index("role")
+    chips = lax.axis_size("dev")
     model_width = moe_rows.shape[1]
-    hidden_width = expert_down.shape[1]
-    half_count = row_count // 2
-    half_slots = max(2, row_count * top_count // expert_count)
-    slot_count = 2 * half_slots
+    swap = [(0, 1), (1, 0)]
+    base = jnp.full((1,), role * chips, jnp.int32)
+    other_ids = lax.ppermute(expert_ids, "role", swap)
+    other_rows = lax.ppermute(moe_rows, "role", swap)
+    other_gates = lax.ppermute(gate_weights, "role", swap)
+    outgoing = place(base, expert_ids, other_ids, moe_rows, other_rows, chips)
+    arrived = lax.all_to_all(
+        outgoing.reshape(chips, -1, model_width), "dev", split_axis=0, concat_axis=0, tiled=True
+    )
+    result = expert(arrived.reshape(-1, model_width), expert_in, expert_down)
+    returned = lax.all_to_all(
+        result.reshape(chips, -1, model_width), "dev", split_axis=0, concat_axis=0, tiled=True
+    )
+    own, other = mix(
+        base,
+        expert_ids,
+        other_ids,
+        gate_weights,
+        other_gates,
+        returned.reshape(-1, model_width),
+        chips,
+    )
+    mixed = (own + lax.ppermute(other, "role", swap).astype(jnp.float32)).astype(jnp.bfloat16)
     attended = attend(queries, key_value_cache, guessed_key_value, cache_length_per_request)
-    chosen = (
-        expert_ids[:, :, None] == jnp.arange(expert_count, dtype=jnp.int32)[None, None, :]
-    ).astype(jnp.int32)
-    member = jnp.sum(chosen, axis=1)
-    halves_view = member.reshape(2, half_count, expert_count)
-    ranks = (jnp.cumsum(halves_view, axis=1) - halves_view).reshape(row_count, expert_count)
-    half_index = (jnp.arange(row_count, dtype=jnp.int32) // half_count)[:, None]
-    slot = half_index * half_slots + ranks
-    placing = (slot.T[:, None, :] == jnp.arange(slot_count, dtype=jnp.int32)[None, :, None]) & (
-        member.T[:, None, :] > 0
-    )
-    outgoing = jnp.einsum(
-        "est,td->esd", placing.astype(jnp.bfloat16), moe_rows, preferred_element_type=jnp.float32
-    ).astype(jnp.bfloat16)
-    block_in = lax.all_to_all(outgoing, ("role", "dev"), split_axis=0, concat_axis=0, tiled=True)
-    rows = block_in.reshape(-1, model_width)
-    joint = jnp.dot(rows, expert_in[0], preferred_element_type=jnp.float32)
-    hidden = (jax.nn.silu(joint[:, :hidden_width]) * joint[:, hidden_width:]).astype(jnp.bfloat16)
-    result = jnp.dot(hidden, expert_down[0], preferred_element_type=jnp.float32).astype(
-        jnp.bfloat16
-    )
-    results = result.reshape(block_in.shape)
-    returned = lax.all_to_all(results, ("role", "dev"), split_axis=0, concat_axis=0, tiled=True)
-    route_weights = gate_weights / jnp.sum(gate_weights, axis=-1, keepdims=True)
-    slot_taken = jnp.take_along_axis(slot, expert_ids, axis=1)
-    flat_index = expert_ids * slot_count + slot_taken
-    picked = returned.reshape(-1, model_width)[flat_index]
-    mixed = jnp.sum(route_weights[:, :, None] * picked.astype(jnp.float32), axis=1)
-    return (attended, mixed.astype(jnp.bfloat16))
+    return (attended, mixed)
 
 
 def solution(mesh):

time: 181 us -> 155 us (0.86)
  local copies, waits for them, and re-layouts: 47 us -> 17.6 us
  Pallas kernels: 0 us -> 20.4 us
  matrix products: 23.3 us -> 3.69 us
  starting transfers between devices: 7.57 us -> 14.4 us
  blocking collectives: 64.5 us -> 62.6 us
  other arithmetic: 3.91 us -> 2.03 us
    reshape x3 -> x0, local copies, waits for them, and re-layouts: 21 us -> none  [the longest x1 7.19 us: body(): results = result.reshape(block_in.shape)]
    pallas_call x0 -> x3, Pallas kernels: none -> 20.4 us  [the longest x1 12.5 us: expert(): pl.pallas_call(expert_kernel, out_shape=pltpu.HBM((row_count, width), jnp...]
    dot_general x3 -> x0, matrix products: 19.6 us -> none  [the longest x1 10.5 us: body(): joint = jnp.dot(rows, expert_in[0], preferred_element_type=jnp.float32)]
    gather x4 -> x0, local copies, waits for them, and re-layouts: 8.72 us -> none  [the longest x1 6.65 us: body(): picked = returned.reshape(-1, model_width)[flat_index]]
    ppermute x0 -> x4, starting transfers between devices: none -> 7.71 us  [the longest x1 4.03 us: body(): lax.ppermute(other, 'role', swap).astype(jnp.float32)]
    unnamed x18 -> x21, local copies, waits for them, and re-layouts: 8.16 us -> 11.9 us
    convert_element_type x1 -> x0, local copies, waits for them, and re-layouts: 3.24 us -> none  [body(): outgoing = jnp.einsum('est,td->esd', placing.astype(jnp.bfloat16), moe_ro...]
    reduce_sum x3 -> x0, other arithmetic: 2.46 us -> none  [the longest x1 2.34 us: body(): jnp.sum(route_weights[:, :, None] * picked.astype(jnp.float32), axis=1)]
  transfers between devices with their start and end apart: 1 -> 5, of which waited for: 1 -> 2; matrix products, arithmetic and copies ran while one was open for 11% -> 12% of each run, Pallas kernels for 0% -> 0%
where the time goes in v1:
time: 155 us; the launch traced here: 154 us
  blocking collectives  62.6 us (40%)
  waiting for transfers between devices  32.8 us (21%)
  Pallas kernels  20.4 us (13%)
  local copies, waits for them, and re-layouts  17.6 us (11%)
  starting transfers between devices  14.4 us (9%)
  matrix products  3.69 us (2%)
  other arithmetic  2.03 us (1%)
    all_to_all x1, blocking collectives, body(): lax.all_to_all(outgoing.reshape(chips, -1, model_width), 'dev', split_axi...  62.6 us
    all_to_all x1, waiting for transfers between devices, body(): lax.all_to_all(result.reshape(chips, -1, model_width), 'dev', split_axis=...  31.6 us
    pallas_call x1, Pallas kernels, expert(): pl.pallas_call(expert_kernel, out_shape=pltpu.HBM((row_count, width), jnp...  12.5 us
    unnamed x21, local copies, waits for them, and re-layouts  11.9 us
    all_to_all x1, starting transfers between devices, body(): lax.all_to_all(result.reshape(chips, -1, model_width), 'dev', split_axis=...  6.7 us
    slice x1, local copies, waits for them, and re-layouts, attend(): key_value_cache[:, :, :feature_width]  4.58 us
    ppermute x1, starting transfers between devices, body(): lax.ppermute(other, 'role', swap).astype(jnp.float32)  4.03 us
    pallas_call x1, Pallas kernels, mix(): pl.pallas_call(functools.partial(mix_kernel, chips), grid=(width // tile,...  4.01 us
  transfers between devices with their start and end apart: 5, of which 2 were waited for; matrix products, arithmetic and copies ran while one was open for 12% of the time, Pallas kernels for 0%

profile of v1, /device:TPU:1, one launch (start us, length us, event | category | flops | bytes accessed | tf_op | source)
XLA Modules:
  0.0 154.3 jit_solution(14250121933341728118)
XLA Ops:
  0.6 1.5 collective-permute-start.2
  2.1 0.8 copy.28.own_ids
  2.9 0.0 collective-permute-start
  2.9 1.2 collective-permute-done.other_ids
  4.1 0.9 copy-done
  5.0 3.9 %place_rows.1 = bf16[512,4096]{1,0:T(8,128)(2,1)} custom-call(s32[1]{0:T(128)} %bitcast.13.base_ref, s32[32,8]{1,0:T(8,128)S(1)} %copy.28.own_ids, s32[32,8]{1,0:T(8,128)S(1)} %collective-permute-done.other_ids, bf16[32,4096]{1,0:T(8,128)(2,1)S(1)} %copy-done, bf16[32,4096]{1,0:T(8,128)(2,1)S(1)} %collective-permute-done.2.other_ref), custom_call_target="tpu_custom_call" | custom-call | tf_op jit(solution)/shard_map/place_rows/pallas_call | solution.py:118
  8.9 62.6 %all_to_all.10 = bf16[64,8,4096]{2,1,0:T(8,128)(2,1)} all-to-all(bf16[64,8,4096]{2,1,0:T(8,128)(2,1)} %bitcast.54), channel_id=1, replica_groups=mesh['role'=2,'dev'=64] {'dev'}, dimensions={0} | all-to-all | bytes 8388608 | tf_op jit(solution)/shard_map/all_to_all | solution.py:278
  71.5 2.8 %copy-done.2 = bf16[1,768,4096]{2,1,0:T(8,128)(2,1)S(1)} copy-done((bf16[1,768,4096]{2,1,0:T(8,128)(2,1)S(1)}, bf16[1,768,4096]{2,1,0:T(8,128)(2,1)}, u32[]{:S(2)}) %copy-start.2) | copy-done | bytes 6291480
  74.3 12.5 %expert_layer.1 = bf16[512,4096]{1,0:T(8,128)(2,1)} custom-call(bf16[512,4096]{1,0:T(8,128)(2,1)} %bitcast.57, bf16[1,4096,1536]{2,1,0:T(8,128)(2,1)S(1)} %copy-done.1, bf16[1,768,4096]{2,1,0:T(8,128)(2,1)S(1)} %copy-done.2), custom_call_target="tpu_custom_call" | custom-call | flops 9663676416 | bytes 8388608 | tf_op jit(solution)/shard_map/expert_layer/pallas_call | solution.py:227
  86.8 0.0 copy-start.6
  86.8 6.7 %all-to-all-start.1 = ((bf16[64,8,4096]{2,1,0:T(8,128)(2,1)}), bf16[64,8,4096]{2,1,0:T(8,128)(2,1)}, u32[]{:S(2)}, u32[]{:S(2)}) async-start(bf16[64,8,4096]{2,1,0:T(8,128)(2,1)} %bitcast.56), calls=%async_computation.1 | async-start | bytes 8388608 | tf_op jit(solution)/shard_map/all_to_all | solution.py:282
  93.6 0.1 copy.29.own_gates
  93.6 2.2 %collective-permute-start.1 = (f32[32,8]{1,0:T(8,128)S(1)}, f32[32,8]{1,0:T(8,128)S(1)}, u32[]{:S(2)}, u32[]{:S(2)}) collective-permute-start(f32[32,8]{1,0:T(8,128)S(1)} %copy.29.own_gates), channel_id=1, source_target_pairs={{0,64},{64,0},{1,65},{65,1},{2,66},{66,2},{3,67},{67,3},{4,68},{68... | collective-permute-start | bytes 3080 | tf_op jit(solution)/shard_map/ppermute | solution.py:276
  95.8 4.6 %fusion.16 = (bf16[8,256,512]{2,1,0:T(8,128)(2,1)}, bf16[8,256,512]{2,1,0:T(8,128)(2,1)}) fusion(bf16[8,256,1024]{2,1,0:T(8,128)(2,1)} %param.10), kind=kLoop, calls=%fused_computation.29 | loop fusion | bytes 8388608 | tf_op jit(solution)/shard_map/slice | solution.py:26
  100.4 2.9 %copy.38 = bf16[8,256,512]{1,2,0:T(8,128)(2,1)S(1)} copy(bf16[8,256,512]{2,1,0:T(8,128)(2,1)} %get-tuple-element.6) | data formatting | bytes 4194304
  103.3 0.1 copy.40
  103.5 0.0 copy-start.7
  103.5 3.9 %copy.39 = bf16[8,256,512]{1,2,0:T(8,128)(2,1)} copy(bf16[8,256,512]{2,1,0:T(8,128)(2,1)} %get-tuple-element.7) | data formatting | bytes 4194304
  107.4 0.1 iota_compare_fusion
  107.5 1.4 fusion.17
  108.9 0.6 bitcast_reduce_fusion
  109.5 0.2 fusion.11
  109.8 0.9 fusion.1
  110.7 0.4 copy-done.3
  111.1 1.3 fusion.6
  112.4 31.6 %all-to-all-done.1 = bf16[64,8,4096]{2,1,0:T(8,128)(2,1)} async-done(((bf16[64,8,4096]{2,1,0:T(8,128)(2,1)}), bf16[64,8,4096]{2,1,0:T(8,128)(2,1)}, u32[]{:S(2)}, u32[]{:S(2)}) %all-to-all-start.1) | async-done | bytes 4194336 | tf_op jit(solution)/shard_map/all_to_all | solution.py:282
  144.1 4.0 %mix_results.1 = (f32[32,4096]{1,0:T(8,128)S(1)}, bf16[32,4096]{1,0:T(8,128)(2,1)S(1)}) custom-call(s32[1]{0:T(128)} %bitcast.13.base_ref, s32[32,8]{1,0:T(8,128)S(1)} %copy.28.own_ids, s32[32,8]{1,0:T(8,128)S(1)} %collective-permute-done.other_ids, f32[32,8]{1,0:T(8,128)S(1)} %copy.29.own_gates, f32[32,8]{1,0:T(8,128)S(1)} %collective-permute-done.1.other_gates, ...), custom_call_target="tpu_custom_call" | custom-call | tf_op jit(solution)/shard_map/mix_results/pallas_call | solution.py:162
  148.1 4.0 %collective-permute-start.3 = (bf16[32,4096]{1,0:T(8,128)(2,1)S(1)}, bf16[32,4096]{1,0:T(8,128)(2,1)S(1)}, u32[]{:S(2)}, u32[]{:S(2)}) collective-permute-start(bf16[32,4096]{1,0:T(8,128)(2,1)S(1)} %get-tuple-element.5), channel_id=1, source_target_pairs={{0,64},{64,0},{1,65},{65,1},{2,66},{66,2},{3,67},{67,3},{4,68},{68... | collective-permute-start | bytes 786440 | tf_op jit(solution)/shard_map/ppermute | solution.py:294
  152.1 0.4 fusion.3
  152.5 0.1 copy.24
  152.6 1.0 convert_element_type.25
  153.6 0.7 add_convert_fusion
  (18 shorter events, 0.1 us)
Async XLA Ops:
  0.6 3.5 %collective-permute-start.2 = (bf16[32,4096]{1,0:T(8,128)(2,1)}, bf16[32,4096]{1,0:T(8,128)(2,1)S(1)}, u32[]{:S(2)}, u32[]{:S(2)}) collective-permute-start(bf16[32,4096]{1,0:T(8,128)(2,1)} %own_ref.1), channel_id=1, source_target_pairs={{0,64},{64,0},{1,65},{65,1},{2,66},{66,2},{3,67},{67,3},{4,68},{68... | collective-permute-start | bytes 786440 | tf_op jit(solution)/shard_map/ppermute | solution.py:275
  2.9 1.2 collective-permute-start
  4.1 1.0 copy-start
  5.0 66.5 %copy-start.1 = (bf16[1,4096,1536]{2,1,0:T(8,128)(2,1)S(1)}, bf16[1,4096,1536]{2,1,0:T(8,128)(2,1)}, u32[]{:S(2)}) copy-start(bf16[1,4096,1536]{2,1,0:T(8,128)(2,1)} %in_ref.1) | copy-start | bytes 37748740
  71.5 2.8 %copy-start.2 = (bf16[1,768,4096]{2,1,0:T(8,128)(2,1)S(1)}, bf16[1,768,4096]{2,1,0:T(8,128)(2,1)}, u32[]{:S(2)}) copy-start(bf16[1,768,4096]{2,1,0:T(8,128)(2,1)} %down_ref.1) | copy-start | bytes 18874372
  86.8 6.7 %copy-start.6 = (f32[32,8]{0,1:T(8,128)S(1)}, f32[32,8]{0,1:T(8,128)}, u32[]{:S(2)}) copy-start(f32[32,8]{0,1:T(8,128)} %param.15) | copy-start | bytes 3076
  86.8 57.2 %all-to-all-start.1 = ((bf16[64,8,4096]{2,1,0:T(8,128)(2,1)}), bf16[64,8,4096]{2,1,0:T(8,128)(2,1)}, u32[]{:S(2)}, u32[]{:S(2)}) async-start(bf16[64,8,4096]{2,1,0:T(8,128)(2,1)} %bitcast.56), calls=%async_computation.1 | async-start | bytes 8388608 | tf_op jit(solution)/shard_map/all_to_all | solution.py:282
  93.6 18.8 %collective-permute-start.1 = (f32[32,8]{1,0:T(8,128)S(1)}, f32[32,8]{1,0:T(8,128)S(1)}, u32[]{:S(2)}, u32[]{:S(2)}) collective-permute-start(f32[32,8]{1,0:T(8,128)S(1)} %copy.29.own_gates), channel_id=1, source_target_pairs={{0,64},{64,0},{1,65},{65,1},{2,66},{66,2},{3,67},{67,3},{4,68},{68... | collective-permute-start | bytes 3080 | tf_op jit(solution)/shard_map/ppermute | solution.py:276
  100.4 2.9 %copy-start.4 = (bf16[32,8192]{1,0:T(8,128)(2,1)S(1)}, bf16[32,8192]{1,0:T(8,128)(2,1)}, u32[]{:S(2)}) copy-start(bf16[32,8192]{1,0:T(8,128)(2,1)} %param.9) | copy-start | bytes 1572868
  100.4 3.1 %copy-start.5 = (bf16[32,1024]{1,0:T(8,128)(2,1)S(1)}, bf16[32,1024]{1,0:T(8,128)(2,1)}, u32[]{:S(2)}) copy-start(bf16[32,1024]{1,0:T(8,128)(2,1)} %param.11) | copy-start | bytes 196612
  103.5 4.0 %copy-start.7 = (s32[8]{0:T(128)S(1)}, s32[8]{0:T(128)}, u32[]{:S(2)}) copy-start(s32[8]{0:T(128)} %param.12) | copy-start | bytes 100
  109.5 1.6 %copy-start.3 = (bf16[8,256,512]{1,2,0:T(8,128)(2,1)S(1)}, bf16[8,256,512]{1,2,0:T(8,128)(2,1)}, u32[]{:S(2)}) copy-start(bf16[8,256,512]{1,2,0:T(8,128)(2,1)} %copy.39) | copy-start | bytes 6291460
  148.1 5.5 %collective-permute-start.3 = (bf16[32,4096]{1,0:T(8,128)(2,1)S(1)}, bf16[32,4096]{1,0:T(8,128)(2,1)S(1)}, u32[]{:S(2)}, u32[]{:S(2)}) collective-permute-start(bf16[32,4096]{1,0:T(8,128)(2,1)S(1)} %get-tuple-element.5), channel_id=1, source_target_pairs={{0,64},{64,0},{1,65},{65,1},{2,66},{66,2},{3,67},{67,3},{4,68},{68... | collective-permute-start | bytes 786440 | tf_op jit(solution)/shard_map/ppermute | solution.py:294

commit v2 on v0

--- a/solution.py
+++ b/solution.py
@@ -1,11 +1,19 @@
+import functools
+
 import jax
 import jax.numpy as jnp
 from jax import lax
+from jax.experimental import pallas as pl
+from jax.experimental.pallas import tpu as pltpu
 from jax.sharding import PartitionSpec as P
 
 QUERY_HEADS = 64
 KEY_VALUE_HEADS = 4
 HEAD_SIZE = 128
+BLOCK_ROWS = 16
+BLOCK_SLOTS = 2
+ROW_PARTS = 2
+COLUMN_PARTS = 4
 
 
 def attend(queries, key_value_cache, guessed_key_value, cache_length_per_request):
@@ -66,6 +74,178 @@
     )
     return output.reshape(request_number * guessed_count, QUERY_HEADS * HEAD_SIZE).astype(
         jnp.bfloat16
+    )
+
+
+def expert_spots(own_ids, other_ids, base, chips):
+    ids = jnp.concatenate([own_ids, other_ids], axis=1)
+    top_count, columns = ids.shape
+    slots = columns // BLOCK_ROWS * BLOCK_SLOTS
+    shape = (chips * slots, columns)
+    line = lax.broadcasted_iota(jnp.int32, shape, 0)
+    column = lax.broadcasted_iota(jnp.int32, shape, 1)
+    serving = base + line // slots
+    matches = [ids[k : k + 1, :] == serving for k in range(top_count)]
+    member = functools.reduce(jnp.logical_or, matches)
+    here = lax.broadcasted_iota(jnp.int32, (columns, columns), 0)
+    there = lax.broadcasted_iota(jnp.int32, (columns, columns), 1)
+    earlier = (here < there) & (here // BLOCK_ROWS == there // BLOCK_ROWS)
+    ranks = jnp.dot(
+        jnp.where(member, 1.0, 0.0).astype(jnp.bfloat16),
+        jnp.where(earlier, 1.0, 0.0).astype(jnp.bfloat16),
+        preferred_element_type=jnp.float32,
+    ).astype(jnp.int32)
+    return matches, member & (column // BLOCK_ROWS * BLOCK_SLOTS + ranks == line % slots)
+
+
+def place_kernel(chips, base_ref, own_ids, other_ids, own_ref, other_ref, out_ref, spots):
+    @pl.when(pl.program_id(0) == 0)
+    def _():
+        _, taken = expert_spots(own_ids[...], other_ids[...], base_ref[0], chips)
+        spots[...] = jnp.where(taken, 1.0, 0.0).astype(jnp.bfloat16)
+
+    rows = jnp.concatenate([own_ref[...], other_ref[...]], axis=0)
+    out_ref[...] = jnp.dot(spots[...], rows, preferred_element_type=jnp.float32).astype(
+        jnp.bfloat16
+    )
+
+
+def place(base, own_ids, other_ids, own, other, chips):
+    row_count, width = own.shape
+    lines = chips * 2 * row_count // BLOCK_ROWS * BLOCK_SLOTS
+    tile = min(width, 1024)
+    whole = pl.BlockSpec(own_ids.shape, lambda i: (0, 0))
+    part = pl.BlockSpec((row_count, tile), lambda i: (0, i))
+    return pl.pallas_call(
+        functools.partial(place_kernel, chips),
+        grid=(width // tile,),
+        out_shape=jax.ShapeDtypeStruct((lines, width), jnp.bfloat16),
+        in_specs=[pl.BlockSpec(memory_space=pltpu.SMEM), whole, whole, part, part],
+        out_specs=pl.BlockSpec((lines, tile), lambda i: (0, i)),
+        scratch_shapes=[pltpu.VMEM((lines, 2 * row_count), jnp.bfloat16)],
+        compiler_params=pltpu.CompilerParams(vmem_limit_bytes=12 << 20),
+        name="place_rows",
+    )(base, own_ids, other_ids, own, other)
+
+
+def weigh_kernel(chips, base_ref, own_ids, other_ids, own_gates, other_gates, out_ref):
+    columns = out_ref.shape[0] // 2
+    matches, taken = expert_spots(own_ids[...], other_ids[...], base_ref[0], chips)
+    gates = jnp.concatenate([own_gates[...], other_gates[...]], axis=1)
+    route = gates / jnp.sum(gates, axis=0, keepdims=True)
+    weight = sum(jnp.where(match, route[k : k + 1, :], 0.0) for k, match in enumerate(matches))
+    weight = jnp.where(taken, weight, 0.0).T
+    high = weight.astype(jnp.bfloat16)
+    out_ref[:columns] = high
+    out_ref[columns:] = (weight - high.astype(jnp.float32)).astype(jnp.bfloat16)
+
+
+def weigh(base, own_ids, other_ids, own_gates, other_gates, lines):
+    vmem = pl.BlockSpec(memory_space=pltpu.VMEM)
+    chips = lines * BLOCK_ROWS // (2 * own_ids.shape[1] * BLOCK_SLOTS)
+    return pl.pallas_call(
+        functools.partial(weigh_kernel, chips),
+        out_shape=jax.ShapeDtypeStruct((4 * own_ids.shape[1], lines), jnp.bfloat16),
+        in_specs=[pl.BlockSpec(memory_space=pltpu.SMEM)] + [vmem] * 4,
+        out_specs=vmem,
+        compiler_params=pltpu.CompilerParams(vmem_limit_bytes=12 << 20),
+        name="weigh_lines",
+    )(base, own_ids, other_ids, own_gates, other_gates)
+
+
+def mix_kernel(spread, in_ref, own_ref, other_ref):
+    row_count = own_ref.shape[0]
+    total = jnp.dot(spread[...], in_ref[...], preferred_element_type=jnp.float32)
+    total = total[: 2 * row_count] + total[2 * row_count :]
+    own_ref[...] = total[:row_count]
+    other_ref[...] = total[row_count:].astype(jnp.bfloat16)
+
+
+def mix(spread, returned):
+    row_count = spread.shape[0] // 4
+    lines, width = returned.shape
+    tile = min(width, 1024)
+    part = pl.BlockSpec((row_count, tile), lambda i: (0, i))
+    return pl.pallas_call(
+        mix_kernel,
+        grid=(width // tile,),
+        out_shape=(
+            jax.ShapeDtypeStruct((row_count, width), jnp.float32),
+            jax.ShapeDtypeStruct((row_count, width), jnp.bfloat16),
+        ),
+        in_specs=[
+            pl.BlockSpec(spread.shape, lambda i: (0, 0)),
+            pl.BlockSpec((lines, tile), lambda i: (0, i)),
+        ],
+        out_specs=(part, part),
+        compiler_params=pltpu.CompilerParams(vmem_limit_bytes=12 << 20),
+        name="mix_results",
+    )(spread, returned)
+
+
+def expert_kernel(rows, in_ref, down_hbm, out_hbm, down, joint, hidden, out, down_sem, out_sems):
+    row_count, width = rows.shape
+    hidden_width = hidden.shape[1]
+    block = row_count // ROW_PARTS
+    cut = width // COLUMN_PARTS
+
+    def leave(part, step):
+        place = (pl.ds(part * block, block), pl.ds(step * cut, cut))
+        return pltpu.make_async_copy(out.at[place], out_hbm.at[place], out_sems.at[part, step])
+
+    fetch = pltpu.make_async_copy(down_hbm, down, down_sem.at[0])
+    fetch.start()
+    for part in range(ROW_PARTS):
+        lines = slice(part * block, (part + 1) * block)
+        joint[lines] = jnp.dot(rows[lines], in_ref[0], preferred_element_type=jnp.float32)
+        gate = joint[lines, :hidden_width]
+        hidden[lines] = (gate / (1.0 + jnp.exp(-gate)) * joint[lines, hidden_width:]).astype(
+            jnp.bfloat16
+        )
+        if part == 0:
+            fetch.wait()
+        for step in range(COLUMN_PARTS):
+            columns = slice(step * cut, (step + 1) * cut)
+            out[lines, columns] = jnp.dot(
+                hidden[lines], down[0, :, columns], preferred_element_type=jnp.float32
+            ).astype(jnp.bfloat16)
+            leave(part, step).start()
+    for part in range(ROW_PARTS):
+        for step in range(COLUMN_PARTS):
+            leave(part, step).wait()
+
+
+def expert(rows, expert_in, expert_down):
+    row_count, width = rows.shape
+    hidden_width = expert_down.shape[1]
+    return pl.pallas_call(
+        expert_kernel,
+        out_shape=pltpu.HBM((row_count, width), jnp.bfloat16),
+        in_specs=[
+            pl.BlockSpec(memory_space=pltpu.VMEM),
+            pl.BlockSpec(memory_space=pltpu.VMEM),
+            pl.BlockSpec(memory_space=pl.ANY),
+        ],
+        out_specs=pl.BlockSpec(memory_space=pl.ANY),
+        scratch_shapes=[
+            pltpu.VMEM(expert_down.shape, jnp.bfloat16),
+            pltpu.VMEM((row_count, 2 * hidden_width), jnp.float32),
+            pltpu.VMEM((row_count, hidden_width), jnp.bfloat16),
+            pltpu.VMEM((row_count, width), jnp.bfloat16),
+            pltpu.SemaphoreType.DMA((1,)),
+            pltpu.SemaphoreType.DMA((ROW_PARTS, COLUMN_PARTS)),
+        ],
+        compiler_params=pltpu.CompilerParams(vmem_limit_bytes=24 << 20),
+        cost_estimate=pl.CostEstimate(
+            flops=6 * row_count * width * hidden_width,
+            bytes_accessed=4 * row_count * width,
+            transcendentals=row_count * hidden_width,
+        ),
+        name="expert_layer",
+    )(
+        pltpu.with_memory_space_constraint(rows, pltpu.VMEM),
+        pltpu.with_memory_space_constraint(expert_in, pltpu.VMEM),
+        pltpu.with_memory_space_constraint(expert_down, pltpu.HBM),
     )
 
 
@@ -80,43 +260,30 @@
     expert_in,
     expert_down,
 ):
-    expert_count = lax.axis_size(("role", "dev"))
-    row_count, top_count = expert_ids.shape
+    role = lax.axis_index("role")
+    chips = lax.axis_size("dev")
     model_width = moe_rows.shape[1]
-    hidden_width = expert_down.shape[1]
-    half_count = row_count // 2
-    half_slots = max(2, row_count * top_count // expert_count)
-    slot_count = 2 * half_slots
+    swap = [(0, 1), (1, 0)]
+    base = jnp.full((1,), role * chips, jnp.int32)
+
+    def exchange(lines):
+        blocks = lines.reshape(chips, -1, model_width)
+        moved = lax.all_to_all(blocks, "dev", split_axis=0, concat_axis=0, tiled=True)
+        return moved.reshape(-1, model_width)
+
+    ids = expert_ids.T
+    other_ids = lax.ppermute(ids, "role", swap)
+    other_rows = lax.ppermute(moe_rows, "role", swap)
+    outgoing = place(base, ids, other_ids, moe_rows, other_rows, chips)
+    outgoing, expert_in = lax.optimization_barrier((outgoing, expert_in))
+    result = expert(exchange(outgoing), expert_in, expert_down)
+    result, gates = lax.optimization_barrier((result, gate_weights.T))
+    other_gates = lax.ppermute(gates, "role", swap)
+    spread = weigh(base, ids, other_ids, gates, other_gates, result.shape[0])
+    own, other = mix(spread, exchange(result))
+    mixed = (own + lax.ppermute(other, "role", swap).astype(jnp.float32)).astype(jnp.bfloat16)
     attended = attend(queries, key_value_cache, guessed_key_value, cache_length_per_request)
-    chosen = (
-        expert_ids[:, :, None] == jnp.arange(expert_count, dtype=jnp.int32)[None, None, :]
-    ).astype(jnp.int32)
-    member = jnp.sum(chosen, axis=1)
-    halves_view = member.reshape(2, half_count, expert_count)
-    ranks = (jnp.cumsum(halves_view, axis=1) - halves_view).reshape(row_count, expert_count)
-    half_index = (jnp.arange(row_count, dtype=jnp.int32) // half_count)[:, None]
-    slot = half_index * half_slots + ranks
-    placing = (slot.T[:, None, :] == jnp.arange(slot_count, dtype=jnp.int32)[None, :, None]) & (
-        member.T[:, None, :] > 0
-    )
-    outgoing = jnp.einsum(
-        "est,td->esd", placing.astype(jnp.bfloat16), moe_rows, preferred_element_type=jnp.float32
-    ).astype(jnp.bfloat16)
-    block_in = lax.all_to_all(outgoing, ("role", "dev"), split_axis=0, concat_axis=0, tiled=True)
-    rows = block_in.reshape(-1, model_width)
-    joint = jnp.dot(rows, expert_in[0], preferred_element_type=jnp.float32)
-    hidden = (jax.nn.silu(joint[:, :hidden_width]) * joint[:, hidden_width:]).astype(jnp.bfloat16)
-    result = jnp.dot(hidden, expert_down[0], preferred_element_type=jnp.float32).astype(
-        jnp.bfloat16
-    )
-    results = result.reshape(block_in.shape)
-    returned = lax.all_to_all(results, ("role", "dev"), split_axis=0, concat_axis=0, tiled=True)
-    route_weights = gate_weights / jnp.sum(gate_weights, axis=-1, keepdims=True)
-    slot_taken = jnp.take_along_axis(slot, expert_ids, axis=1)
-    flat_index = expert_ids * slot_count + slot_taken
-    picked = returned.reshape(-1, model_width)[flat_index]
-    mixed = jnp.sum(route_weights[:, :, None] * picked.astype(jnp.float32), axis=1)
-    return (attended, mixed.astype(jnp.bfloat16))
+    return (attended, mixed)
 
 
 def solution(mesh):

time: 181 us -> 148 us (0.82)
  local copies, waits for them, and re-layouts: 47 us -> 14.3 us
  matrix products: 23.3 us -> 3.72 us
  Pallas kernels: 0 us -> 17.6 us
  starting transfers between devices: 7.57 us -> 14.8 us
  blocking collectives: 64.5 us -> 61.8 us
  other arithmetic: 3.91 us -> 2.02 us
    reshape x3 -> x0, local copies, waits for them, and re-layouts: 21 us -> none  [the longest x1 7.19 us: body(): results = result.reshape(block_in.shape)]
    dot_general x3 -> x0, matrix products: 19.6 us -> none  [the longest x1 10.5 us: body(): joint = jnp.dot(rows, expert_in[0], preferred_element_type=jnp.float32)]
    pallas_call x0 -> x4, Pallas kernels: none -> 17.6 us  [the longest x1 11 us: expert(): pl.pallas_call(expert_kernel, out_shape=pltpu.HBM((row_count, width), jnp...]
    gather x4 -> x0, local copies, waits for them, and re-layouts: 8.72 us -> none  [the longest x1 6.65 us: body(): picked = returned.reshape(-1, model_width)[flat_index]]
    ppermute x0 -> x4, starting transfers between devices: none -> 7.51 us  [the longest x1 3.76 us: body(): lax.ppermute(other, 'role', swap).astype(jnp.float32)]
    convert_element_type x1 -> x0, local copies, waits for them, and re-layouts: 3.24 us -> none  [body(): outgoing = jnp.einsum('est,td->esd', placing.astype(jnp.bfloat16), moe_ro...]
    all_to_all x1, blocking collectives: 64.5 us -> 61.8 us  [exchange(): lax.all_to_all(blocks, 'dev', split_axis=0, concat_axis=0, tiled=True)]
    reduce_sum x3 -> x0, other arithmetic: 2.46 us -> none  [the longest x1 2.34 us: body(): jnp.sum(route_weights[:, :, None] * picked.astype(jnp.float32), axis=1)]
  transfers between devices with their start and end apart: 1 -> 5, of which waited for: 1 -> 2; matrix products, arithmetic and copies ran while one was open for 11% -> 12% of each run, Pallas kernels for 0% -> 0%
where the time goes in v2:
time: 148 us
  blocking collectives  61.8 us (42%)
  waiting for transfers between devices  32.7 us (22%)
  Pallas kernels  17.6 us (12%)
  starting transfers between devices  14.8 us (10%)
  local copies, waits for them, and re-layouts  14.3 us (10%)
  matrix products  3.72 us (3%)
  other arithmetic  2.02 us (1%)
    all_to_all x1, blocking collectives, exchange(): lax.all_to_all(blocks, 'dev', split_axis=0, concat_axis=0, tiled=True)  61.8 us
    all_to_all x1, waiting for transfers between devices, exchange(): lax.all_to_all(blocks, 'dev', split_axis=0, concat_axis=0, tiled=True)  31.4 us
    pallas_call x1, Pallas kernels, expert(): pl.pallas_call(expert_kernel, out_shape=pltpu.HBM((row_count, width), jnp...  11 us
    unnamed x21, local copies, waits for them, and re-layouts  8.62 us
    all_to_all x1, starting transfers between devices, exchange(): lax.all_to_all(blocks, 'dev', split_axis=0, concat_axis=0, tiled=True)  7.29 us
    slice x1, local copies, waits for them, and re-layouts, attend(): key_value_cache[:, :, :feature_width]  4.57 us
    ppermute x1, starting transfers between devices, body(): lax.ppermute(other, 'role', swap).astype(jnp.float32)  3.76 us
    pallas_call x1, Pallas kernels, mix(): pl.pallas_call(mix_kernel, grid=(width // tile,), out_shape=(jax.ShapeDty...  3.54 us
  transfers between devices with their start and end apart: 5, of which 2 were waited for; matrix products, arithmetic and copies ran while one was open for 12% of the time, Pallas kernels for 0%

profile of v2, /device:TPU:1, one launch (start us, length us, event | category | flops | bytes accessed | tf_op | source)
XLA Modules:
  0.0 147.7 jit_solution(4375605526963114831)
XLA Ops:
  0.6 1.5 %collective-permute-start.1 = (bf16[32,4096]{1,0:T(8,128)(2,1)}, bf16[32,4096]{1,0:T(8,128)(2,1)S(1)}, u32[]{:S(2)}, u32[]{:S(2)}) collective-permute-start(bf16[32,4096]{1,0:T(8,128)(2,1)} %own_ref.1), channel_id=1, source_target_pairs={{0,64},{64,0},{1,65},{65,1},{2,66},{66,2},{3,67},{67,3},{4,68},{68... | collective-permute-start | bytes 786440 | tf_op jit(solution)/shard_map/ppermute | solution.py:276
  2.1 0.1 collective-permute-start
  2.2 1.3 collective-permute-done.other_ids
  3.5 0.0 collective-permute-done.1.other_ref
  3.5 0.9 copy-done
  4.5 0.7 copy-done.1
  5.2 2.4 %place_rows.1 = bf16[512,4096]{1,0:T(8,128)(2,1)S(1)} custom-call(s32[1]{0:T(128)} %bitcast.13.base_ref, s32[8,32]{1,0:T(8,128)S(1)} %bitcast.59, s32[8,32]{1,0:T(8,128)S(1)} %collective-permute-done.other_ids, bf16[32,4096]{1,0:T(8,128)(2,1)S(1)} %copy-done, bf16[32,4096]{1,0:T(8,128)(2,1)S(1)} %collective-permute-done.1.other_ref), custom_call_target="tpu_custom_call" | custom-call | tf_op jit(solution)/shard_map/place_rows/pallas_call | solution.py:119
  7.6 61.8 %all_to_all.10 = bf16[64,8,4096]{2,1,0:T(8,128)(2,1)S(1)} all-to-all(bf16[64,8,4096]{2,1,0:T(8,128)(2,1)S(1)} %bitcast.56), channel_id=1, replica_groups=mesh['role'=2,'dev'=64] {'dev'}, dimensions={0} | all-to-all | bytes 8388608 | tf_op jit(solution)/shard_map/all_to_all | solution.py:271
  69.4 11.0 %expert_layer.1 = bf16[512,4096]{1,0:T(8,128)(2,1)} custom-call(bf16[512,4096]{1,0:T(8,128)(2,1)S(1)} %bitcast.57, bf16[1,4096,1536]{2,1,0:T(8,128)(2,1)S(1)} %copy-done.4, bf16[1,768,4096]{2,1,0:T(8,128)(2,1)} %down_hbm.1), custom_call_target="tpu_custom_call" | custom-call | flops 9663676416 | bytes 8388608 | tf_op jit(solution)/shard_map/expert_layer/pallas_call | solution.py:221
  80.4 7.3 %all-to-all-start.1 = ((bf16[64,8,4096]{2,1,0:T(8,128)(2,1)}), bf16[64,8,4096]{2,1,0:T(8,128)(2,1)}, u32[]{:S(2)}, u32[]{:S(2)}) async-start(bf16[64,8,4096]{2,1,0:T(8,128)(2,1)} %bitcast.64), calls=%async_computation.1 | async-start | bytes 8388608 | tf_op jit(solution)/shard_map/all_to_all | solution.py:271
  87.7 4.6 %fusion.16 = (bf16[8,256,512]{2,1,0:T(8,128)(2,1)}, bf16[8,256,512]{2,1,0:T(8,128)(2,1)}) fusion(bf16[8,256,1024]{2,1,0:T(8,128)(2,1)} %param.10), kind=kLoop, calls=%fused_computation.29 | loop fusion | bytes 8388608 | tf_op jit(solution)/shard_map/slice | solution.py:28
  92.3 2.9 %copy.28 = bf16[8,256,512]{1,2,0:T(8,128)(2,1)S(1)} copy(bf16[8,256,512]{2,1,0:T(8,128)(2,1)} %get-tuple-element.14) | data formatting | bytes 4194304
  95.2 0.1 copy.30
  95.4 0.0 copy-start.8
  95.4 3.9 %copy.29 = bf16[8,256,512]{1,2,0:T(8,128)(2,1)} copy(bf16[8,256,512]{2,1,0:T(8,128)(2,1)} %get-tuple-element.15) | data formatting | bytes 4194304
  99.3 0.1 iota_compare_fusion
  99.4 1.4 fusion.17
  100.8 0.6 bitcast_reduce_fusion
  101.4 0.0 copy-start.3
  101.4 0.3 fusion.11
  101.7 0.9 fusion.1
  102.6 2.2 %collective-permute-start.2 = (f32[8,32]{1,0:T(8,128)S(1)}, f32[8,32]{1,0:T(8,128)S(1)}, u32[]{:S(2)}, u32[]{:S(2)}) collective-permute-start(f32[8,32]{1,0:T(8,128)S(1)} %bitcast.61), channel_id=1, source_target_pairs={{0,64},{64,0},{1,65},{65,1},{2,66},{66,2},{3,67},{67,3},{4,68},{68... | collective-permute-start | bytes 3080 | tf_op jit(solution)/shard_map/ppermute | solution.py:281
  104.8 1.4 fusion.6
  106.2 0.0 collective-permute-done.2.other_gates
  106.2 0.6 weigh_lines.1.spread
  106.8 31.4 %all-to-all-done.1 = bf16[64,8,4096]{2,1,0:T(8,128)(2,1)} async-done(((bf16[64,8,4096]{2,1,0:T(8,128)(2,1)}), bf16[64,8,4096]{2,1,0:T(8,128)(2,1)}, u32[]{:S(2)}, u32[]{:S(2)}) %all-to-all-start.1) | async-done | bytes 4194336 | tf_op jit(solution)/shard_map/all_to_all | solution.py:271
  138.2 3.5 %mix_results.1 = (f32[32,4096]{1,0:T(8,128)S(1)}, bf16[32,4096]{1,0:T(8,128)(2,1)S(1)}) custom-call(bf16[128,512]{1,0:T(8,128)(2,1)S(1)} %weigh_lines.1.spread, bf16[512,4096]{1,0:T(8,128)(2,1)} %bitcast.19.in_ref), custom_call_target="tpu_custom_call" | custom-call | tf_op jit(solution)/shard_map/mix_results/pallas_call | solution.py:169
  141.8 3.8 %collective-permute-start.3 = (bf16[32,4096]{1,0:T(8,128)(2,1)S(1)}, bf16[32,4096]{1,0:T(8,128)(2,1)S(1)}, u32[]{:S(2)}, u32[]{:S(2)}) collective-permute-start(bf16[32,4096]{1,0:T(8,128)(2,1)S(1)} %get-tuple-element.13), channel_id=1, source_target_pairs={{0,64},{64,0},{1,65},{65,1},{2,66},{66,2},{3,67},{67,3},{4,68},{68... | collective-permute-start | bytes 786440 | tf_op jit(solution)/shard_map/ppermute | solution.py:284
  145.5 0.4 fusion.3
  145.9 0.1 copy.19
  146.0 1.0 convert_element_type.25
  147.0 0.7 add_convert_fusion
  (19 shorter events, 0.1 us)
Async XLA Ops:
  0.6 2.9 %collective-permute-start.1 = (bf16[32,4096]{1,0:T(8,128)(2,1)}, bf16[32,4096]{1,0:T(8,128)(2,1)S(1)}, u32[]{:S(2)}, u32[]{:S(2)}) collective-permute-start(bf16[32,4096]{1,0:T(8,128)(2,1)} %own_ref.1), channel_id=1, source_target_pairs={{0,64},{64,0},{1,65},{65,1},{2,66},{66,2},{3,67},{67,3},{4,68},{68... | collective-permute-start | bytes 786440 | tf_op jit(solution)/shard_map/ppermute | solution.py:276
  2.1 1.4 collective-permute-start
  3.5 1.0 copy-start
  4.5 0.7 copy-start.1
  5.2 64.2 %copy-start.4 = (bf16[1,4096,1536]{2,1,0:T(8,128)(2,1)S(1)}, bf16[1,4096,1536]{2,1,0:T(8,128)(2,1)}, u32[]{:S(2)}) copy-start(bf16[1,4096,1536]{2,1,0:T(8,128)(2,1)} %in_ref) | copy-start | bytes 37748740
  80.4 57.8 %all-to-all-start.1 = ((bf16[64,8,4096]{2,1,0:T(8,128)(2,1)}), bf16[64,8,4096]{2,1,0:T(8,128)(2,1)}, u32[]{:S(2)}, u32[]{:S(2)}) async-start(bf16[64,8,4096]{2,1,0:T(8,128)(2,1)} %bitcast.64), calls=%async_computation.1 | async-start | bytes 8388608 | tf_op jit(solution)/shard_map/all_to_all | solution.py:271
  92.3 2.9 %copy-start.6 = (bf16[32,8192]{1,0:T(8,128)(2,1)S(1)}, bf16[32,8192]{1,0:T(8,128)(2,1)}, u32[]{:S(2)}) copy-start(bf16[32,8192]{1,0:T(8,128)(2,1)} %param.9) | copy-start | bytes 1572868
  92.3 3.1 %copy-start.7 = (bf16[32,1024]{1,0:T(8,128)(2,1)S(1)}, bf16[32,1024]{1,0:T(8,128)(2,1)}, u32[]{:S(2)}) copy-start(bf16[32,1024]{1,0:T(8,128)(2,1)} %param.11) | copy-start | bytes 196612
  95.4 3.9 %copy-start.8 = (s32[8]{0:T(128)S(1)}, s32[8]{0:T(128)}, u32[]{:S(2)}) copy-start(s32[8]{0:T(128)} %param.12) | copy-start | bytes 100
  101.4 1.2 copy-start.3
  101.4 3.4 %copy-start.5 = (bf16[8,256,512]{1,2,0:T(8,128)(2,1)S(1)}, bf16[8,256,512]{1,2,0:T(8,128)(2,1)}, u32[]{:S(2)}) copy-start(bf16[8,256,512]{1,2,0:T(8,128)(2,1)} %copy.29) | copy-start | bytes 6291460
  102.6 3.5 %collective-permute-start.2 = (f32[8,32]{1,0:T(8,128)S(1)}, f32[8,32]{1,0:T(8,128)S(1)}, u32[]{:S(2)}, u32[]{:S(2)}) collective-permute-start(f32[8,32]{1,0:T(8,128)S(1)} %bitcast.61), channel_id=1, source_target_pairs={{0,64},{64,0},{1,65},{65,1},{2,66},{66,2},{3,67},{67,3},{4,68},{68... | collective-permute-start | bytes 3080 | tf_op jit(solution)/shard_map/ppermute | solution.py:281
  104.8 1.4 copy-start.2
  141.8 5.2 %collective-permute-start.3 = (bf16[32,4096]{1,0:T(8,128)(2,1)S(1)}, bf16[32,4096]{1,0:T(8,128)(2,1)S(1)}, u32[]{:S(2)}, u32[]{:S(2)}) collective-permute-start(bf16[32,4096]{1,0:T(8,128)(2,1)S(1)} %get-tuple-element.13), channel_id=1, source_target_pairs={{0,64},{64,0},{1,65},{65,1},{2,66},{66,2},{3,67},{67,3},{4,68},{68... | collective-permute-start | bytes 786440 | tf_op jit(solution)/shard_map/ppermute | solution.py:284

commit v3 on v2

--- a/solution.py
+++ b/solution.py
@@ -14,6 +14,7 @@
 BLOCK_SLOTS = 2
 ROW_PARTS = 2
 COLUMN_PARTS = 4
+MIX_PARTS = 8
 
 
 def attend(queries, key_value_cache, guessed_key_value, cache_length_per_request):
@@ -98,34 +99,50 @@
     return matches, member & (column // BLOCK_ROWS * BLOCK_SLOTS + ranks == line % slots)
 
 
-def place_kernel(chips, base_ref, own_ids, other_ids, own_ref, other_ref, out_ref, spots):
-    @pl.when(pl.program_id(0) == 0)
-    def _():
-        _, taken = expert_spots(own_ids[...], other_ids[...], base_ref[0], chips)
-        spots[...] = jnp.where(taken, 1.0, 0.0).astype(jnp.bfloat16)
-
-    rows = jnp.concatenate([own_ref[...], other_ref[...]], axis=0)
-    out_ref[...] = jnp.dot(spots[...], rows, preferred_element_type=jnp.float32).astype(
-        jnp.bfloat16
-    )
+def place_kernel(chips, base_ref, own_ids, other_ids, own_hbm, other_ref, out_ref, rows, row_sem):
+    row_count, width = own_hbm.shape
+    fetch = pltpu.make_async_copy(own_hbm, rows, row_sem.at[0])
+    fetch.start()
+    _, taken = expert_spots(own_ids[...], other_ids[...], base_ref[0], chips)
+    spots = jnp.where(taken, 1.0, 0.0).astype(jnp.bfloat16)
+    fetch.wait()
+    cut = width // COLUMN_PARTS
+    for step in range(COLUMN_PARTS):
+        columns = slice(step * cut, (step + 1) * cut)
+        both = jnp.concatenate([rows[:, columns], other_ref[:, columns]], axis=0)
+        out_ref[:, columns] = jnp.dot(spots, both, preferred_element_type=jnp.float32).astype(
+            jnp.bfloat16
+        )
 
 
 def place(base, own_ids, other_ids, own, other, chips):
     row_count, width = own.shape
     lines = chips * 2 * row_count // BLOCK_ROWS * BLOCK_SLOTS
-    tile = min(width, 1024)
-    whole = pl.BlockSpec(own_ids.shape, lambda i: (0, 0))
-    part = pl.BlockSpec((row_count, tile), lambda i: (0, i))
+    vmem = pl.BlockSpec(memory_space=pltpu.VMEM)
     return pl.pallas_call(
         functools.partial(place_kernel, chips),
-        grid=(width // tile,),
-        out_shape=jax.ShapeDtypeStruct((lines, width), jnp.bfloat16),
-        in_specs=[pl.BlockSpec(memory_space=pltpu.SMEM), whole, whole, part, part],
-        out_specs=pl.BlockSpec((lines, tile), lambda i: (0, i)),
-        scratch_shapes=[pltpu.VMEM((lines, 2 * row_count), jnp.bfloat16)],
+        out_shape=pltpu.VMEM((lines, width), jnp.bfloat16),
+        in_specs=[
+            pl.BlockSpec(memory_space=pltpu.SMEM),
+            vmem,
+            vmem,
+            pl.BlockSpec(memory_space=pl.ANY),
+            vmem,
+        ],
+        out_specs=vmem,
+        scratch_shapes=[
+            pltpu.VMEM((row_count, width), jnp.bfloat16),
+            pltpu.SemaphoreType.DMA((1,)),
+        ],
         compiler_params=pltpu.CompilerParams(vmem_limit_bytes=12 << 20),
         name="place_rows",
-    )(base, own_ids, other_ids, own, other)
+    )(
+        base,
+        own_ids,
+        other_ids,
+        pltpu.with_memory_space_constraint(own, pltpu.HBM),
+        pltpu.with_memory_space_constraint(other, pltpu.VMEM),
+    )
 
 
 def weigh_kernel(chips, base_ref, own_ids, other_ids, own_gates, other_gates, out_ref):
@@ -153,34 +170,44 @@
     )(base, own_ids, other_ids, own_gates, other_gates)
 
 
-def mix_kernel(spread, in_ref, own_ref, other_ref):
-    row_count = own_ref.shape[0]
-    total = jnp.dot(spread[...], in_ref[...], preferred_element_type=jnp.float32)
-    total = total[: 2 * row_count] + total[2 * row_count :]
-    own_ref[...] = total[:row_count]
-    other_ref[...] = total[row_count:].astype(jnp.bfloat16)
+def mix_kernel(spread, in_hbm, own_ref, other_ref, lines, line_sems):
+    row_count, width = own_ref.shape
+    cut = width // MIX_PARTS
+
+    def arrive(step):
+        columns = pl.ds(step * cut, cut)
+        return pltpu.make_async_copy(in_hbm.at[:, columns], lines.at[step], line_sems.at[step])
+
+    for step in range(MIX_PARTS):
+        arrive(step).start()
+    for step in range(MIX_PARTS):
+        arrive(step).wait()
+        columns = slice(step * cut, (step + 1) * cut)
+        total = jnp.dot(spread[...], lines[step], preferred_element_type=jnp.float32)
+        total = total[: 2 * row_count] + total[2 * row_count :]
+        own_ref[:, columns] = total[:row_count]
+        other_ref[:, columns] = total[row_count:].astype(jnp.bfloat16)
 
 
 def mix(spread, returned):
     row_count = spread.shape[0] // 4
     lines, width = returned.shape
-    tile = min(width, 1024)
-    part = pl.BlockSpec((row_count, tile), lambda i: (0, i))
+    vmem = pl.BlockSpec(memory_space=pltpu.VMEM)
     return pl.pallas_call(
         mix_kernel,
-        grid=(width // tile,),
         out_shape=(
             jax.ShapeDtypeStruct((row_count, width), jnp.float32),
             jax.ShapeDtypeStruct((row_count, width), jnp.bfloat16),
         ),
-        in_specs=[
-            pl.BlockSpec(spread.shape, lambda i: (0, 0)),
-            pl.BlockSpec((lines, tile), lambda i: (0, i)),
-        ],
-        out_specs=(part, part),
+        in_specs=[vmem, pl.BlockSpec(memory_space=pl.ANY)],
+        out_specs=(vmem, vmem),
+        scratch_shapes=[
+            pltpu.VMEM((MIX_PARTS, lines, width // MIX_PARTS), jnp.bfloat16),
+            pltpu.SemaphoreType.DMA((MIX_PARTS,)),
+        ],
         compiler_params=pltpu.CompilerParams(vmem_limit_bytes=12 << 20),
         name="mix_results",
-    )(spread, returned)
+    )(spread, pltpu.with_memory_space_constraint(returned, pltpu.HBM))
 
 
 def expert_kernel(rows, in_ref, down_hbm, out_hbm, down, joint, hidden, out, down_sem, out_sems):
@@ -271,18 +298,33 @@
         moved = lax.all_to_all(blocks, "dev", split_axis=0, concat_axis=0, tiled=True)
         return moved.reshape(-1, model_width)
 
-    ids = expert_ids.T
+    ids, gates = expert_ids.T, gate_weights.T
     other_ids = lax.ppermute(ids, "role", swap)
     other_rows = lax.ppermute(moe_rows, "role", swap)
+    other_gates = lax.ppermute(gates, "role", swap)
+    asked = (queries, key_value_cache, guessed_key_value, cache_length_per_request)
+    attended = lax.cond(role == 1, attend, lambda queries, *_: jnp.zeros_like(queries), *asked)
+    other_rows, other_gates, attended = lax.optimization_barrier(
+        (other_rows, other_gates, attended)
+    )
     outgoing = place(base, ids, other_ids, moe_rows, other_rows, chips)
     outgoing, expert_in = lax.optimization_barrier((outgoing, expert_in))
     result = expert(exchange(outgoing), expert_in, expert_down)
-    result, gates = lax.optimization_barrier((result, gate_weights.T))
-    other_gates = lax.ppermute(gates, "role", swap)
+    result, queries = lax.optimization_barrier((result, queries))
+    returned = exchange(result)
     spread = weigh(base, ids, other_ids, gates, other_gates, result.shape[0])
-    own, other = mix(spread, exchange(result))
-    mixed = (own + lax.ppermute(other, "role", swap).astype(jnp.float32)).astype(jnp.bfloat16)
-    attended = attend(queries, key_value_cache, guessed_key_value, cache_length_per_request)
+    attended = lax.cond(
+        role == 0,
+        lambda done, *asked: attend(*asked),
+        lambda done, *_: done,
+        attended,
+        queries,
+        *asked[1:],
+    )
+    returned, spread, attended = lax.optimization_barrier((returned, spread, attended))
+    own, other = mix(spread, returned)
+    received = lax.ppermute(other, "role", swap)
+    mixed = (own + received.astype(jnp.float32)).astype(jnp.bfloat16)
     return (attended, mixed)
 
 

time: 148 us -> 136 us (0.919)
  blocking collectives: 61.8 us -> 48.1 us
  waiting for transfers between devices: 32.7 us -> 43.1 us
  starting transfers between devices: 14.8 us -> 7.9 us
  local copies, waits for them, and re-layouts: 14.3 us -> 12 us
    all_to_all x1, blocking collectives: 61.8 us -> 48.1 us  [exchange(): lax.all_to_all(blocks, 'dev', split_axis=0, concat_axis=0, tiled=True)]
    all_to_all x1, waiting for transfers between devices: 31.4 us -> 41.6 us  [exchange(): lax.all_to_all(blocks, 'dev', split_axis=0, concat_axis=0, tiled=True)]
    unnamed x21 -> x12, local copies, waits for them, and re-layouts: 8.62 us -> 0.04 us
    another operation x0 -> x1, local copies, waits for them, and re-layouts: none -> 6.49 us
    ppermute x1, starting transfers between devices: 3.76 us -> 0.09 us  [body(): received = lax.ppermute(other, 'role', swap)]
    ppermute x1, starting transfers between devices: 2.16 us -> 0.09 us  [body(): other_gates = lax.ppermute(gates, 'role', swap)]
    ppermute x1, waiting for transfers between devices: 0.01 us -> 1.52 us  [body(): received = lax.ppermute(other, 'role', swap)]
    all_to_all x1, starting transfers between devices: 7.29 us -> 5.8 us  [exchange(): lax.all_to_all(blocks, 'dev', split_axis=0, concat_axis=0, tiled=True)]
  transfers between devices with their start and end apart: 5 -> 5, of which waited for: 2 -> 2; matrix products, arithmetic and copies ran while one was open for 12% -> 13% of each run, Pallas kernels for 0% -> 0%
where the time goes in v3:
time: 136 us
  blocking collectives  48.1 us (35%)
  waiting for transfers between devices  43.1 us (32%)
  Pallas kernels  17.1 us (13%)
  local copies, waits for them, and re-layouts  12 us (9%)
  starting transfers between devices  7.9 us (6%)
  matrix products  3.74 us (3%)
  other arithmetic  2.7 us (2%)
    all_to_all x1, blocking collectives, exchange(): lax.all_to_all(blocks, 'dev', split_axis=0, concat_axis=0, tiled=True)  48.1 us
    all_to_all x1, waiting for transfers between devices, exchange(): lax.all_to_all(blocks, 'dev', split_axis=0, concat_axis=0, tiled=True)  41.6 us
    pallas_call x1, Pallas kernels, expert(): pl.pallas_call(expert_kernel, out_shape=pltpu.HBM((row_count, width), jnp...  11.2 us
    another operation x1, local copies, waits for them, and re-layouts  6.49 us
    all_to_all x1, starting transfers between devices, exchange(): lax.all_to_all(blocks, 'dev', split_axis=0, concat_axis=0, tiled=True)  5.8 us
    slice x1, local copies, waits for them, and re-layouts, attend(): key_value_cache[:, :, :feature_width]  3.96 us
    pallas_call x1, Pallas kernels, mix(): pl.pallas_call(mix_kernel, out_shape=(jax.ShapeDtypeStruct((row_count, wi...  3 us
  transfers between devices with their start and end apart: 5, of which 2 were waited for; matrix products, arithmetic and copies ran while one was open for 13% of the time, Pallas kernels for 0%

profile of v3, /device:TPU:1, one launch (start us, length us, event | category | flops | bytes accessed | tf_op | source)
XLA Modules:
  0.0 135.7 jit_solution(5371034778094393893)
XLA Ops:
  0.6 1.5 %collective-permute-start.1 = (bf16[32,4096]{1,0:T(8,128)(2,1)}, bf16[32,4096]{1,0:T(8,128)(2,1)S(1)}, u32[]{:S(2)}, u32[]{:S(2)}) collective-permute-start(bf16[32,4096]{1,0:T(8,128)(2,1)} %own_hbm.1), channel_id=1, source_target_pairs={{0,64},{64,0},{1,65},{65,1},{2,66},{66,2},{3,67},{67,3},{4,68},{68... | collective-permute-start | bytes 786440 | tf_op jit(solution)/shard_map/ppermute | solution.py:303
  2.1 0.1 collective-permute-start.2
  2.2 0.4 collective-permute-start
  2.6 17.7 %conditional.2 = (bf16[32,8192]{1,0:T(8,128)(2,1)}) conditional(s32[]{:T(128)} %convert_element_type.42, () %tuple.24, (s32[8]{0:T(128)}, bf16[8,256,1024]{2,1,0:T(8,128)(2,1)}, bf16[32,8192]{1,0:T(8,128)(2,1)}, bf16[32,1024]{1,0:T(8,128)(2,1)}) %tuple.25), branch_computations={%region_0.0_spmd, %region_1.6_spmd} | conditional | flops 279508992 | bytes 45605516 | solution.py:306
  2.6 0.7 iota_compare_fusion
  3.4 6.5 %copy.25 = bf16[8,256,1024]{1,2,0:T(8,128)(2,1)} copy(bf16[8,256,1024]{2,1,0:T(8,128)(2,1)} %get-tuple-element.58) | data formatting | bytes 8388608 | tf_op jit(solution)/shard_map
  9.9 4.0 %fusion.32 = (bf16[8,256,512]{1,2,0:T(8,128)(2,1)S(1)}, bf16[8,256,512]{1,2,0:T(8,128)(2,1)}) fusion(bf16[8,256,1024]{1,2,0:T(8,128)(2,1)} %copy.25), kind=kLoop, calls=%fused_computation.57 | loop fusion | bytes 8388608 | tf_op jit(solution)/shard_map/cond/branch_1_fun/slice | solution.py:29
  13.8 0.1 copy.43
  14.0 0.0 copy-start.8
  14.0 0.6 bitcast_reduce_fusion
  14.6 0.2 copy-done.8
  14.9 1.4 %fusion.33 = (f32[8,4,4,16]{3,1,2,0:T(4,128)S(1)}, f32[8,4,4,16,4]{3,4,1,2,0:T(4,128)S(1)}) fusion(bf16[8,4,4,16,128]{4,3,2,1,0:T(8,128)(2,1)S(1)} %bitcast.116, bf16[8,4,1024]{2,1,0:T(4,128)(2,1)S(1)} %reshape.124, pred[4,4]{1,0:T(4,128)(4,1)S(1)} %iota_compare_fusion.1), kind=kOutput, calls=%fused_computation.58 | convolution fusion | flops 2119680 | bytes 598528 | tf_op jit(solution)/shard_map/cond/branch_1_fun/rsngd,rjnd->rsngj/dot_general | solution.py:49
  16.3 0.9 fusion.1
  17.2 0.2 fusion.11
  17.5 1.4 %fusion.6 = f32[8,4,4,16,128]{4,3,2,1,0:T(8,128)S(1)} fusion(bf16[8,256,4,128,1]{1,3,4,2,0:T(8,128)(2,1)S(1)} %bitcast.121, f32[8,4,256,4,16]{2,4,3,1,0:T(8,128)S(1)} %get-tuple-element.68, f32[8,4,4,16]{3,1,2,0:T(4,128)S(1)} %add.22, f32[8,4,4,16]{3,1,2,0:T(4,128)S(1)} %max.14, pred[8,256]{1,0:T(8,128)(4,1)S(1)} %iota_compare_fusion), kind=kOutput, calls=%fused_computation.12 | convolution fusion | flops 136839168 | bytes 5261312 | tf_op jit(solution)/shard_map/cond/branch_1_fun/rsngc,rcnd->rsngd/dot_general | solution.py:70
  18.9 0.4 fusion.3
  19.3 0.1 copy.19
  19.3 1.0 convert_element_type.32
  20.4 0.0 copy-start.2
  20.4 2.4 %place_rows.1 = bf16[512,4096]{1,0:T(8,128)(2,1)S(1)} custom-call(s32[1]{0:T(128)} %bitcast.26.base_ref, s32[8,32]{1,0:T(8,128)S(1)} %bitcast.108, s32[8,32]{1,0:T(8,128)S(1)} %collective-permute-done.other_ids, bf16[32,4096]{1,0:T(8,128)(2,1)} %own_hbm.1, bf16[32,4096]{1,0:T(8,128)(2,1)S(1)} %collective-permute-done.1.other_ref), custom_call_target="tpu_custom_call" | custom-call | tf_op jit(solution)/shard_map/place_rows/pallas_call | solution.py:122
  22.7 48.1 %all_to_all.10 = bf16[64,8,4096]{2,1,0:T(8,128)(2,1)S(1)} all-to-all(bf16[64,8,4096]{2,1,0:T(8,128)(2,1)S(1)} %bitcast.105), channel_id=1, replica_groups=mesh['role'=2,'dev'=64] {'dev'}, dimensions={0} | all-to-all | bytes 8388608 | tf_op jit(solution)/shard_map/all_to_all | solution.py:298
  70.8 11.2 %expert_layer.1 = bf16[512,4096]{1,0:T(8,128)(2,1)} custom-call(bf16[512,4096]{1,0:T(8,128)(2,1)S(1)} %bitcast.106, bf16[1,4096,1536]{2,1,0:T(8,128)(2,1)S(1)} %copy-done.2, bf16[1,768,4096]{2,1,0:T(8,128)(2,1)} %down_hbm.1), custom_call_target="tpu_custom_call" | custom-call | flops 9663676416 | bytes 8388608 | tf_op jit(solution)/shard_map/expert_layer/pallas_call | solution.py:248
  82.0 0.0 copy-start.3
  82.0 0.0 copy-start.7
  82.0 5.8 %all-to-all-start.1 = ((bf16[64,8,4096]{2,1,0:T(8,128)(2,1)}), bf16[64,8,4096]{2,1,0:T(8,128)(2,1)}, u32[]{:S(2)}, u32[]{:S(2)}) async-start(bf16[64,8,4096]{2,1,0:T(8,128)(2,1)} %bitcast.114), calls=%async_computation.1 | async-start | bytes 8388608 | tf_op jit(solution)/shard_map/all_to_all | solution.py:298
  87.9 0.6 weigh_lines.1.spread
  88.5 0.2 conditional.3
  88.7 41.6 %all-to-all-done.1 = bf16[64,8,4096]{2,1,0:T(8,128)(2,1)} async-done(((bf16[64,8,4096]{2,1,0:T(8,128)(2,1)}), bf16[64,8,4096]{2,1,0:T(8,128)(2,1)}, u32[]{:S(2)}, u32[]{:S(2)}) %all-to-all-start.1) | async-done | bytes 4194336 | tf_op jit(solution)/shard_map/all_to_all | solution.py:298
  130.4 3.0 %mix_results.1 = (f32[32,4096]{1,0:T(8,128)S(1)}, bf16[32,4096]{1,0:T(8,128)(2,1)S(1)}) custom-call(bf16[128,512]{1,0:T(8,128)(2,1)S(1)} %weigh_lines.1.spread, bf16[512,4096]{1,0:T(8,128)(2,1)} %bitcast.32.in_hbm), custom_call_target="tpu_custom_call" | custom-call | tf_op jit(solution)/shard_map/mix_results/pallas_call | solution.py:196
  133.4 0.1 collective-permute-start.3
  133.5 1.5 %collective-permute-done.3 = bf16[32,4096]{1,0:T(8,128)(2,1)S(1)} collective-permute-done((bf16[32,4096]{1,0:T(8,128)(2,1)S(1)}, bf16[32,4096]{1,0:T(8,128)(2,1)S(1)}, u32[]{:S(2)}, u32[]{:S(2)}) %collective-permute-start.3) | collective-permute-done | bytes 262176 | tf_op jit(solution)/shard_map/ppermute | solution.py:326
  135.0 0.7 add_convert_fusion
  (20 shorter events, 0.1 us)
Async XLA Ops:
  0.6 19.7 %collective-permute-start.1 = (bf16[32,4096]{1,0:T(8,128)(2,1)}, bf16[32,4096]{1,0:T(8,128)(2,1)S(1)}, u32[]{:S(2)}, u32[]{:S(2)}) collective-permute-start(bf16[32,4096]{1,0:T(8,128)(2,1)} %own_hbm.1), channel_id=1, source_target_pairs={{0,64},{64,0},{1,65},{65,1},{2,66},{66,2},{3,67},{67,3},{4,68},{68... | collective-permute-start | bytes 786440 | tf_op jit(solution)/shard_map/ppermute | solution.py:303
  2.1 18.2 %collective-permute-start.2 = (f32[8,32]{1,0:T(8,128)}, f32[8,32]{1,0:T(8,128)S(1)}, u32[]{:S(2)}, u32[]{:S(2)}) collective-permute-start(f32[8,32]{1,0:T(8,128)} %bitcast.110), channel_id=1, source_target_pairs={{0,64},{64,0},{1,65},{65,1},{2,66},{66,2},{3,67},{67,3},{4,68},{68... | collective-permute-start | bytes 3080 | tf_op jit(solution)/shard_map/ppermute | solution.py:304
  2.2 18.1 %collective-permute-start = (s32[8,32]{1,0:T(8,128)}, s32[8,32]{1,0:T(8,128)S(1)}, u32[]{:S(2)}, u32[]{:S(2)}) collective-permute-start(s32[8,32]{1,0:T(8,128)} %bitcast.107), channel_id=1, source_target_pairs={{0,64},{64,0},{1,65},{65,1},{2,66},{66,2},{3,67},{67,3},{4,68},{68... | collective-permute-start | bytes 3080 | tf_op jit(solution)/shard_map/ppermute | solution.py:302
  2.6 17.7 %copy-start = (s32[32,8]{0,1:T(8,128)S(1)}, s32[32,8]{0,1:T(8,128)}, u32[]{:S(2)}) copy-start(s32[32,8]{0,1:T(8,128)} %param.18) | copy-start | bytes 3076
  9.9 4.0 %copy-start.4 = (bf16[32,8192]{1,0:T(8,128)(2,1)S(1)}, bf16[32,8192]{1,0:T(8,128)(2,1)}, u32[]{:S(2)}) copy-start(bf16[32,8192]{1,0:T(8,128)(2,1)} %get-tuple-element.25) | copy-start | bytes 1572868 | tf_op jit(solution)/shard_map/cond
  14.0 0.8 copy-start.8
  14.8 2.6 %copy-start.5 = (bf16[8,256,512]{1,2,0:T(8,128)(2,1)S(1)}, bf16[8,256,512]{1,2,0:T(8,128)(2,1)}, u32[]{:S(2)}) copy-start(bf16[8,256,512]{1,2,0:T(8,128)(2,1)} %get-tuple-element.66) | copy-start | bytes 6291460 | tf_op jit(solution)/shard_map/cond
  20.4 50.4 %copy-start.2 = (bf16[1,4096,1536]{2,1,0:T(8,128)(2,1)S(1)}, bf16[1,4096,1536]{2,1,0:T(8,128)(2,1)}, u32[]{:S(2)}) copy-start(bf16[1,4096,1536]{2,1,0:T(8,128)(2,1)} %in_ref) | copy-start | bytes 37748740
  82.0 5.9 %copy-start.1 = (f32[32,8]{0,1:T(8,128)S(1)}, f32[32,8]{0,1:T(8,128)}, u32[]{:S(2)}) copy-start(f32[32,8]{0,1:T(8,128)} %param.19) | copy-start | bytes 3076
  82.0 6.5 %copy-start.3 = (bf16[32,8192]{1,0:T(8,128)(2,1)S(1)}, bf16[32,8192]{1,0:T(8,128)(2,1)}, u32[]{:S(2)}) copy-start(bf16[32,8192]{1,0:T(8,128)(2,1)} %param.13) | copy-start | bytes 1572868
  82.0 6.5 %copy-start.7 = (bf16[32,1024]{1,0:T(8,128)(2,1)S(1)}, bf16[32,1024]{1,0:T(8,128)(2,1)}, u32[]{:S(2)}) copy-start(bf16[32,1024]{1,0:T(8,128)(2,1)} %param.15) | copy-start | bytes 196612
  82.0 6.5 %copy-start.9 = (s32[8]{0:T(128)S(1)}, s32[8]{0:T(128)}, u32[]{:S(2)}) copy-start(s32[8]{0:T(128)} %param.16) | copy-start | bytes 100
  82.0 48.3 %all-to-all-start.1 = ((bf16[64,8,4096]{2,1,0:T(8,128)(2,1)}), bf16[64,8,4096]{2,1,0:T(8,128)(2,1)}, u32[]{:S(2)}, u32[]{:S(2)}) async-start(bf16[64,8,4096]{2,1,0:T(8,128)(2,1)} %bitcast.114), calls=%async_computation.1 | async-start | bytes 8388608 | tf_op jit(solution)/shard_map/all_to_all | solution.py:298
  133.4 1.6 %collective-permute-start.3 = (bf16[32,4096]{1,0:T(8,128)(2,1)S(1)}, bf16[32,4096]{1,0:T(8,128)(2,1)S(1)}, u32[]{:S(2)}, u32[]{:S(2)}) collective-permute-start(bf16[32,4096]{1,0:T(8,128)(2,1)S(1)} %get-tuple-element.56), channel_id=1, source_target_pairs={{0,64},{64,0},{1,65},{65,1},{2,66},{66,2},{3,67},{67,3},{4,68},{68... | collective-permute-start | bytes 786440 | tf_op jit(solution)/shard_map/ppermute | solution.py:326

commit v4 on v3

--- a/solution.py
+++ b/solution.py
@@ -14,7 +14,8 @@
 BLOCK_SLOTS = 2
 ROW_PARTS = 2
 COLUMN_PARTS = 4
-MIX_PARTS = 8
+MIX_PARTS = 4
+ATTEND_CUTS = (2, 4)
 
 
 def attend(queries, key_value_cache, guessed_key_value, cache_length_per_request):
@@ -76,6 +77,23 @@
     return output.reshape(request_number * guessed_count, QUERY_HEADS * HEAD_SIZE).astype(
         jnp.bfloat16
     )
+
+
+def attend_in_groups(queries, key_value_cache, guessed_key_value, cache_length_per_request):
+    arrays = (queries, key_value_cache, guessed_key_value, cache_length_per_request)
+    requests = key_value_cache.shape[0]
+    groups = zip(
+        *(
+            jnp.split(array, [cut * array.shape[0] // requests for cut in ATTEND_CUTS])
+            for array in arrays
+        )
+    )
+    done = []
+    for group in groups:
+        if done:
+            done[-1], group = lax.optimization_barrier((done[-1], group))
+        done.append(attend(*group))
+    return jnp.concatenate(done)
 
 
 def expert_spots(own_ids, other_ids, base, chips):
@@ -303,7 +321,9 @@
     other_rows = lax.ppermute(moe_rows, "role", swap)
     other_gates = lax.ppermute(gates, "role", swap)
     asked = (queries, key_value_cache, guessed_key_value, cache_length_per_request)
-    attended = lax.cond(role == 1, attend, lambda queries, *_: jnp.zeros_like(queries), *asked)
+    attended = lax.cond(
+        role == 1, attend_in_groups, lambda queries, *_: jnp.zeros_like(queries), *asked
+    )
     other_rows, other_gates, attended = lax.optimization_barrier(
         (other_rows, other_gates, attended)
     )
@@ -315,7 +335,7 @@
     spread = weigh(base, ids, other_ids, gates, other_gates, result.shape[0])
     attended = lax.cond(
         role == 0,
-        lambda done, *asked: attend(*asked),
+        lambda done, *asked: attend_in_groups(*asked),
         lambda done, *_: done,
         attended,
         queries,

time: 136 us -> 132 us (0.971)
  waiting for transfers between devices: 43.1 us -> 39 us
  blocking collectives: 48.1 us -> 44.9 us
  matrix products: 3.74 us -> 6.92 us
    all_to_all x1, waiting for transfers between devices: 41.6 us -> 37.4 us  [exchange(): lax.all_to_all(blocks, 'dev', split_axis=0, concat_axis=0, tiled=True)]
    all_to_all x1, blocking collectives: 48.1 us -> 44.9 us  [exchange(): lax.all_to_all(blocks, 'dev', split_axis=0, concat_axis=0, tiled=True)]
    dot_general x1 -> x3, matrix products: 1.38 us -> 3.53 us  [attend(): jnp.einsum('rsngc,rcnd->rsngd', probs_cache, cache_value_rows, preferred_...]
    slice x1 -> x3, local copies, waits for them, and re-layouts: 3.96 us -> 4.05 us  [attend(): key_value_cache[:, :, feature_width:]]
  transfers between devices with their start and end apart: 5 -> 5, of which waited for: 2 -> 2; matrix products, arithmetic and copies ran while one was open for 13% -> 16% of each run, Pallas kernels for 0% -> 0%
where the time goes in v4:
time: 132 us; the launch traced here: 131 us
  blocking collectives  44.9 us (34%)
  waiting for transfers between devices  39 us (30%)
  Pallas kernels  16.7 us (13%)
  local copies, waits for them, and re-layouts  11.2 us (8%)
  starting transfers between devices  7.9 us (6%)
  matrix products  6.92 us (5%)
  other arithmetic  3.15 us (2%)
    all_to_all x1, blocking collectives, exchange(): lax.all_to_all(blocks, 'dev', split_axis=0, concat_axis=0, tiled=True)  44.9 us
    all_to_all x1, waiting for transfers between devices, exchange(): lax.all_to_all(blocks, 'dev', split_axis=0, concat_axis=0, tiled=True)  37.4 us
    pallas_call x1, Pallas kernels, expert(): pl.pallas_call(expert_kernel, out_shape=pltpu.HBM((row_count, width), jnp...  11.2 us
    another operation x1, local copies, waits for them, and re-layouts  6.51 us
    all_to_all x1, starting transfers between devices, exchange(): lax.all_to_all(blocks, 'dev', split_axis=0, concat_axis=0, tiled=True)  5.8 us
    slice x3, local copies, waits for them, and re-layouts, attend(): key_value_cache[:, :, feature_width:]  4.05 us
    dot_general x3, matrix products, attend(): jnp.einsum('rsngc,rcnd->rsngd', probs_cache, cache_value_rows, preferred_...  3.53 us
  transfers between devices with their start and end apart: 5, of which 2 were waited for; matrix products, arithmetic and copies ran while one was open for 16% of the time, Pallas kernels for 0%

profile of v4, /device:TPU:1, one launch (start us, length us, event | category | flops | bytes accessed | tf_op | source)
XLA Modules:
  0.0 131.1 jit_solution(13271857553133031248)
XLA Ops:
  0.6 1.5 %collective-permute-start.1 = (bf16[32,4096]{1,0:T(8,128)(2,1)}, bf16[32,4096]{1,0:T(8,128)(2,1)S(1)}, u32[]{:S(2)}, u32[]{:S(2)}) collective-permute-start(bf16[32,4096]{1,0:T(8,128)(2,1)} %own_hbm.1), channel_id=1, source_target_pairs={{0,64},{64,0},{1,65},{65,1},{2,66},{66,2},{3,67},{67,3},{4,68},{68... | collective-permute-start | bytes 786440 | tf_op jit(solution)/shard_map/ppermute | solution.py:321
  2.2 0.4 collective-permute-start
  2.6 20.9 %conditional.2 = (bf16[32,8192]{1,0:T(8,128)(2,1)}) conditional(s32[]{:T(128)} %convert_element_type.102, () %tuple.28, (s32[8]{0:T(128)}, bf16[8,256,1024]{2,1,0:T(8,128)(2,1)}, bf16[32,8192]{1,0:T(8,128)(2,1)}, bf16[32,1024]{1,0:T(8,128)(2,1)}) %tuple.29), branch_computations={%region_0.0_spmd, %region_1.14_spmd} | conditional | flops 278984704 | bytes 55171180 | solution.py:324
  2.7 6.5 %copy.49 = bf16[8,256,1024]{1,2,0:T(8,128)(2,1)} copy(bf16[8,256,1024]{2,1,0:T(8,128)(2,1)} %get-tuple-element.78) | data formatting | bytes 8388608 | tf_op jit(solution)/shard_map
  9.2 2.1 %fusion.90 = (bf16[2,256,512]{1,2,0:T(8,128)(2,1)}, bf16[2,256,512]{1,2,0:T(8,128)(2,1)S(1)}) fusion(bf16[8,256,1024]{1,2,0:T(8,128)(2,1)} %copy.49), kind=kLoop, calls=%fused_computation.157 | loop fusion | bytes 2097152 | tf_op jit(solution)/shard_map/cond/branch_1_fun/slice | solution.py:33
  11.4 0.3 fusion.96
  11.8 0.4 fusion.97
  12.4 0.3 fusion.21
  12.7 0.2 fusion.39
  12.9 1.4 %fusion.11 = bf16[2,4,4,16,128]{4,3,1,2,0:T(8,128)(2,1)S(1)} fusion(f32[2,4,4,16,128]{4,3,2,1,0:T(8,128)S(1)} %fusion.39, bf16[2,256,4,128,1]{1,3,4,2,0:T(8,128)(2,1)} %bitcast.279, f32[2,4,4,16,256]{4,3,1,2,0:T(8,128)S(1)} %get-tuple-element.98, f32[2,4,4,16]{3,1,2,0:T(4,128)S(1)} %add.62, f32[2,4,4,16]{3,1,2,0:T(4,128)S(1)} %max.42), kind=kOutput, calls=%fused_computation.17 | convolution fusion | flops 34078720 | bytes 1445888 | tf_op jit(solution)/shard_map/cond/branch_1_fun/rsngc,rcnd->rsngd/dot_general | solution.py:71
  14.4 0.9 fusion.92
  15.3 0.3 fusion.98
  15.7 0.4 fusion.99
  16.2 0.3 fusion.22
  16.5 0.2 fusion.40
  16.8 1.7 %fusion.10 = bf16[2,4,4,16,128]{4,3,1,2,0:T(8,128)(2,1)S(1)} fusion(f32[2,4,128,4,16]{2,4,3,1,0:T(8,128)S(1)} %fusion.40, bf16[2,256,4,128,1]{1,3,4,2,0:T(8,128)(2,1)} %bitcast.281, f32[2,4,4,16,256]{4,3,1,2,0:T(8,128)} %copy-done.5, f32[2,4,4,16]{3,1,2,0:T(4,128)S(1)} %add.64, f32[2,4,4,16]{3,1,2,0:T(4,128)S(1)} %max.43), kind=kOutput, calls=%fused_computation.16 | convolution fusion | flops 34078720 | bytes 1445888 | tf_op jit(solution)/shard_map/cond/branch_1_fun/rsngc,rcnd->rsngd/dot_general | solution.py:71
  18.7 1.1 fusion.91
  19.9 0.4 fusion.100
  20.4 0.8 fusion.101
  21.3 0.4 fusion.18
  21.7 0.3 fusion.34
  22.0 0.5 fusion.7
  22.6 0.8 pad_maximum_fusion
  23.5 2.3 %place_rows.1 = bf16[512,4096]{1,0:T(8,128)(2,1)S(1)} custom-call(s32[1]{0:T(128)} %bitcast.78.base_ref, s32[8,32]{1,0:T(8,128)S(1)} %bitcast.258, s32[8,32]{1,0:T(8,128)S(1)} %collective-permute-done.other_ids, bf16[32,4096]{1,0:T(8,128)(2,1)} %own_hbm.1, bf16[32,4096]{1,0:T(8,128)(2,1)S(1)} %collective-permute-done.1.other_ref), custom_call_target="tpu_custom_call" | custom-call | tf_op jit(solution)/shard_map/place_rows/pallas_call | solution.py:140
  25.9 44.9 %all_to_all.10 = bf16[64,8,4096]{2,1,0:T(8,128)(2,1)S(1)} all-to-all(bf16[64,8,4096]{2,1,0:T(8,128)(2,1)S(1)} %bitcast.255), channel_id=1, replica_groups=mesh['role'=2,'dev'=64] {'dev'}, dimensions={0} | all-to-all | bytes 8388608 | tf_op jit(solution)/shard_map/all_to_all | solution.py:316
  70.8 11.2 %expert_layer.1 = bf16[512,4096]{1,0:T(8,128)(2,1)} custom-call(bf16[512,4096]{1,0:T(8,128)(2,1)S(1)} %bitcast.256, bf16[1,4096,1536]{2,1,0:T(8,128)(2,1)S(1)} %copy-done.2, bf16[1,768,4096]{2,1,0:T(8,128)(2,1)} %down_hbm.1), custom_call_target="tpu_custom_call" | custom-call | flops 9663676416 | bytes 8388608 | tf_op jit(solution)/shard_map/expert_layer/pallas_call | solution.py:266
  82.0 5.8 %all-to-all-start.1 = ((bf16[64,8,4096]{2,1,0:T(8,128)(2,1)}), bf16[64,8,4096]{2,1,0:T(8,128)(2,1)}, u32[]{:S(2)}, u32[]{:S(2)}) async-start(bf16[64,8,4096]{2,1,0:T(8,128)(2,1)} %bitcast.262), calls=%async_computation.1 | async-start | bytes 8388608 | tf_op jit(solution)/shard_map/all_to_all | solution.py:316
  87.8 0.6 weigh_lines.1.spread
  88.7 37.4 %all-to-all-done.1 = bf16[64,8,4096]{2,1,0:T(8,128)(2,1)} async-done(((bf16[64,8,4096]{2,1,0:T(8,128)(2,1)}), bf16[64,8,4096]{2,1,0:T(8,128)(2,1)}, u32[]{:S(2)}, u32[]{:S(2)}) %all-to-all-start.1) | async-done | bytes 4194336 | tf_op jit(solution)/shard_map/all_to_all | solution.py:316
  126.2 2.5 %mix_results.1 = (f32[32,4096]{1,0:T(8,128)S(1)}, bf16[32,4096]{1,0:T(8,128)(2,1)S(1)}) custom-call(bf16[128,512]{1,0:T(8,128)(2,1)S(1)} %weigh_lines.1.spread, bf16[512,4096]{1,0:T(8,128)(2,1)} %bitcast.84.in_hbm), custom_call_target="tpu_custom_call" | custom-call | tf_op jit(solution)/shard_map/mix_results/pallas_call | solution.py:214
  128.8 1.5 %collective-permute-done.3 = bf16[32,4096]{1,0:T(8,128)(2,1)S(1)} collective-permute-done((bf16[32,4096]{1,0:T(8,128)(2,1)S(1)}, bf16[32,4096]{1,0:T(8,128)(2,1)S(1)}, u32[]{:S(2)}, u32[]{:S(2)}) %collective-permute-start.3) | collective-permute-done | bytes 262176 | tf_op jit(solution)/shard_map/ppermute | solution.py:346
  130.3 0.7 add_convert_fusion
  (65 shorter events, 1.7 us)
Async XLA Ops:
  0.6 22.9 %collective-permute-start.1 = (bf16[32,4096]{1,0:T(8,128)(2,1)}, bf16[32,4096]{1,0:T(8,128)(2,1)S(1)}, u32[]{:S(2)}, u32[]{:S(2)}) collective-permute-start(bf16[32,4096]{1,0:T(8,128)(2,1)} %own_hbm.1), channel_id=1, source_target_pairs={{0,64},{64,0},{1,65},{65,1},{2,66},{66,2},{3,67},{67,3},{4,68},{68... | collective-permute-start | bytes 786440 | tf_op jit(solution)/shard_map/ppermute | solution.py:321
  2.1 21.4 %collective-permute-start.2 = (f32[8,32]{1,0:T(8,128)}, f32[8,32]{1,0:T(8,128)S(1)}, u32[]{:S(2)}, u32[]{:S(2)}) collective-permute-start(f32[8,32]{1,0:T(8,128)} %bitcast.260), channel_id=1, source_target_pairs={{0,64},{64,0},{1,65},{65,1},{2,66},{66,2},{3,67},{67,3},{4,68},{68... | collective-permute-start | bytes 3080 | tf_op jit(solution)/shard_map/ppermute | solution.py:322
  2.2 21.3 %collective-permute-start = (s32[8,32]{1,0:T(8,128)}, s32[8,32]{1,0:T(8,128)S(1)}, u32[]{:S(2)}, u32[]{:S(2)}) collective-permute-start(s32[8,32]{1,0:T(8,128)} %bitcast.257), channel_id=1, source_target_pairs={{0,64},{64,0},{1,65},{65,1},{2,66},{66,2},{3,67},{67,3},{4,68},{68... | collective-permute-start | bytes 3080 | tf_op jit(solution)/shard_map/ppermute | solution.py:320
  2.6 20.9 %copy-start = (s32[32,8]{0,1:T(8,128)S(1)}, s32[32,8]{0,1:T(8,128)}, u32[]{:S(2)}) copy-start(s32[32,8]{0,1:T(8,128)} %param.18) | copy-start | bytes 3076
  2.6 8.6 %copy-start.4 = (bf16[32,8192]{1,0:T(8,128)(2,1)S(1)}, bf16[32,8192]{1,0:T(8,128)(2,1)}, u32[]{:S(2)}) copy-start(bf16[32,8192]{1,0:T(8,128)(2,1)} %get-tuple-element.25) | copy-start | bytes 1572868 | tf_op jit(solution)/shard_map/cond
  2.6 8.6 %copy-start.9 = (s32[8]{0:T(128)S(1)}, s32[8]{0:T(128)}, u32[]{:S(2)}) copy-start(s32[8]{0:T(128)} %get-tuple-element.18) | copy-start | bytes 100 | tf_op jit(solution)/shard_map/cond
  2.6 9.1 %copy-start.7 = (bf16[32,1024]{1,0:T(8,128)(2,1)S(1)}, bf16[32,1024]{1,0:T(8,128)(2,1)}, u32[]{:S(2)}) copy-start(bf16[32,1024]{1,0:T(8,128)(2,1)} %get-tuple-element.26) | copy-start | bytes 196612 | tf_op jit(solution)/shard_map/cond
  11.3 3.1 %slice-start = ((bf16[8,256,1024]{1,2,0:T(8,128)(2,1)}), bf16[2,256,1024]{1,2,0:T(8,128)(2,1)S(1)}, s32[]{:S(2)}) async-start(bf16[8,256,1024]{1,2,0:T(8,128)(2,1)} %copy.49), calls=%async_computation.2 | async-start | bytes 2097152 | tf_op jit(solution)/shard_map/cond/branch_1_fun/split | solution.py:87
  11.8 3.9 %copy-start.10 = (pred[4,4]{1,0:T(4,128)(4,1)}, pred[4,4]{1,0:T(4,128)(4,1)S(1)}, u32[]{:S(2)}) copy-start(pred[4,4]{1,0:T(4,128)(4,1)S(1)} %iota_compare_fusion.2) | copy-start | bytes 52 | tf_op jit(solution)/shard_map/cond
  15.6 0.9 copy-start.5
  16.8 1.9 %slice-start.1 = ((bf16[8,256,1024]{1,2,0:T(8,128)(2,1)}), bf16[4,256,1024]{1,2,0:T(8,128)(2,1)S(1)}, s32[]{:S(2)}) async-start(bf16[8,256,1024]{1,2,0:T(8,128)(2,1)} %copy.49), calls=%async_computation.3 | async-start | bytes 4194304 | tf_op jit(solution)/shard_map/cond/branch_1_fun/split | solution.py:87
  18.6 1.8 %copy-start.11 = (pred[4,4]{1,0:T(4,128)(4,1)S(1)}, pred[4,4]{1,0:T(4,128)(4,1)}, u32[]{:S(2)}) copy-start(pred[4,4]{1,0:T(4,128)(4,1)} %copy-done.10) | copy-start | bytes 52 | tf_op jit(solution)/shard_map/cond
  19.9 2.2 %copy-start.6 = (bf16[4,256,512]{1,2,0:T(8,128)(2,1)S(1)}, bf16[4,256,512]{1,2,0:T(8,128)(2,1)}, u32[]{:S(2)}) copy-start(bf16[4,256,512]{1,2,0:T(8,128)(2,1)} %get-tuple-element.87) | copy-start | bytes 3145732 | tf_op jit(solution)/shard_map/cond
  23.5 47.3 %copy-start.2 = (bf16[1,4096,1536]{2,1,0:T(8,128)(2,1)S(1)}, bf16[1,4096,1536]{2,1,0:T(8,128)(2,1)}, u32[]{:S(2)}) copy-start(bf16[1,4096,1536]{2,1,0:T(8,128)(2,1)} %in_ref) | copy-start | bytes 37748740
  82.0 5.9 %copy-start.1 = (f32[32,8]{0,1:T(8,128)S(1)}, f32[32,8]{0,1:T(8,128)}, u32[]{:S(2)}) copy-start(f32[32,8]{0,1:T(8,128)} %param.19) | copy-start | bytes 3076
  82.0 6.5 %copy-start.3 = (bf16[32,8192]{1,0:T(8,128)(2,1)S(1)}, bf16[32,8192]{1,0:T(8,128)(2,1)}, u32[]{:S(2)}) copy-start(bf16[32,8192]{1,0:T(8,128)(2,1)} %param.13) | copy-start | bytes 1572868
  82.0 6.5 %copy-start.8 = (s32[8]{0:T(128)S(1)}, s32[8]{0:T(128)}, u32[]{:S(2)}) copy-start(s32[8]{0:T(128)} %param.16) | copy-start | bytes 100
  82.0 44.1 %all-to-all-start.1 = ((bf16[64,8,4096]{2,1,0:T(8,128)(2,1)}), bf16[64,8,4096]{2,1,0:T(8,128)(2,1)}, u32[]{:S(2)}, u32[]{:S(2)}) async-start(bf16[64,8,4096]{2,1,0:T(8,128)(2,1)} %bitcast.262), calls=%async_computation.1 | async-start | bytes 8388608 | tf_op jit(solution)/shard_map/all_to_all | solution.py:316
  128.7 1.6 %collective-permute-start.3 = (bf16[32,4096]{1,0:T(8,128)(2,1)S(1)}, bf16[32,4096]{1,0:T(8,128)(2,1)S(1)}, u32[]{:S(2)}, u32[]{:S(2)}) collective-permute-start(bf16[32,4096]{1,0:T(8,128)(2,1)S(1)} %get-tuple-element.76), channel_id=1, source_target_pairs={{0,64},{64,0},{1,65},{65,1},{2,66},{66,2},{3,67},{67,3},{4,68},{68... | collective-permute-start | bytes 786440 | tf_op jit(solution)/shard_map/ppermute | solution.py:346

commit v5 on v4

--- a/solution.py
+++ b/solution.py
@@ -117,36 +117,45 @@
     return matches, member & (column // BLOCK_ROWS * BLOCK_SLOTS + ranks == line % slots)
 
 
-def place_kernel(chips, base_ref, own_ids, other_ids, own_hbm, other_ref, out_ref, rows, row_sem):
-    row_count, width = own_hbm.shape
+def spots_kernel(chips, base_ref, own_ids, other_ids, out_ref):
+    _, taken = expert_spots(own_ids[...], other_ids[...], base_ref[0], chips)
+    out_ref[...] = jnp.where(taken, 1.0, 0.0).astype(jnp.bfloat16)
+
+
+def find_spots(base, own_ids, other_ids, chips):
+    columns = 2 * own_ids.shape[1]
+    lines = chips * columns // BLOCK_ROWS * BLOCK_SLOTS
+    vmem = pl.BlockSpec(memory_space=pltpu.VMEM)
+    return pl.pallas_call(
+        functools.partial(spots_kernel, chips),
+        out_shape=pltpu.VMEM((lines, columns), jnp.bfloat16),
+        in_specs=[pl.BlockSpec(memory_space=pltpu.SMEM), vmem, vmem],
+        out_specs=vmem,
+        compiler_params=pltpu.CompilerParams(vmem_limit_bytes=8 << 20),
+        name="find_spots",
+    )(base, own_ids, other_ids)
+
+
+def place_kernel(spots, own_hbm, other_ref, out_ref, rows, row_sem):
     fetch = pltpu.make_async_copy(own_hbm, rows, row_sem.at[0])
     fetch.start()
-    _, taken = expert_spots(own_ids[...], other_ids[...], base_ref[0], chips)
-    spots = jnp.where(taken, 1.0, 0.0).astype(jnp.bfloat16)
     fetch.wait()
-    cut = width // COLUMN_PARTS
+    cut = rows.shape[1] // COLUMN_PARTS
     for step in range(COLUMN_PARTS):
         columns = slice(step * cut, (step + 1) * cut)
         both = jnp.concatenate([rows[:, columns], other_ref[:, columns]], axis=0)
-        out_ref[:, columns] = jnp.dot(spots, both, preferred_element_type=jnp.float32).astype(
-            jnp.bfloat16
-        )
-
-
-def place(base, own_ids, other_ids, own, other, chips):
+        out_ref[:, columns] = jnp.dot(
+            spots[...], both, preferred_element_type=jnp.float32
+        ).astype(jnp.bfloat16)
+
+
+def place(spots, own, other):
     row_count, width = own.shape
-    lines = chips * 2 * row_count // BLOCK_ROWS * BLOCK_SLOTS
     vmem = pl.BlockSpec(memory_space=pltpu.VMEM)
     return pl.pallas_call(
-        functools.partial(place_kernel, chips),
-        out_shape=pltpu.VMEM((lines, width), jnp.bfloat16),
-        in_specs=[
-            pl.BlockSpec(memory_space=pltpu.SMEM),
-            vmem,
-            vmem,
-            pl.BlockSpec(memory_space=pl.ANY),
-            vmem,
-        ],
+        place_kernel,
+        out_shape=pltpu.VMEM((spots.shape[0], width), jnp.bfloat16),
+        in_specs=[vmem, pl.BlockSpec(memory_space=pl.ANY), vmem],
         out_specs=vmem,
         scratch_shapes=[
             pltpu.VMEM((row_count, width), jnp.bfloat16),
@@ -155,9 +164,7 @@
         compiler_params=pltpu.CompilerParams(vmem_limit_bytes=12 << 20),
         name="place_rows",
     )(
-        base,
-        own_ids,
-        other_ids,
+        spots,
         pltpu.with_memory_space_constraint(own, pltpu.HBM),
         pltpu.with_memory_space_constraint(other, pltpu.VMEM),
     )
@@ -324,10 +331,11 @@
     attended = lax.cond(
         role == 1, attend_in_groups, lambda queries, *_: jnp.zeros_like(queries), *asked
     )
-    other_rows, other_gates, attended = lax.optimization_barrier(
-        (other_rows, other_gates, attended)
-    )
-    outgoing = place(base, ids, other_ids, moe_rows, other_rows, chips)
+    spots = find_spots(base, ids, other_ids, chips)
+    spots, other_rows, other_gates, attended = lax.optimization_barrier(
+        (spots, other_rows, other_gates, attended)
+    )
+    outgoing = place(spots, moe_rows, other_rows)
     outgoing, expert_in = lax.optimization_barrier((outgoing, expert_in))
     result = expert(exchange(outgoing), expert_in, expert_down)
     result, queries = lax.optimization_barrier((result, queries))

time: 132 us -> 133 us (level)
    pallas_call x1 -> x2, Pallas kernels: 2.35 us -> 2.8 us  [the longest x1 2.35 us: place(): pl.pallas_call(place_kernel, out_shape=pltpu.VMEM((spots.shape[0], width)...]
  transfers between devices with their start and end apart: 5 -> 5, of which waited for: 2 -> 2; matrix products, arithmetic and copies ran while one was open for 16% -> 15% of each run, Pallas kernels for 0% -> 1%
where the time goes in v5:
time: 133 us
  blocking collectives  44.8 us (34%)
  waiting for transfers between devices  40.2 us (30%)
  Pallas kernels  17 us (13%)
  local copies, waits for them, and re-layouts  11.2 us (8%)
  starting transfers between devices  7.9 us (6%)
  matrix products  6.94 us (5%)
  other arithmetic  3.15 us (2%)
    all_to_all x1, blocking collectives, exchange(): lax.all_to_all(blocks, 'dev', split_axis=0, concat_axis=0, tiled=True)  44.8 us
    all_to_all x1, waiting for transfers between devices, exchange(): lax.all_to_all(blocks, 'dev', split_axis=0, concat_axis=0, tiled=True)  38.7 us
    pallas_call x1, Pallas kernels, expert(): pl.pallas_call(expert_kernel, out_shape=pltpu.HBM((row_count, width), jnp...  11 us
    another operation x1, local copies, waits for them, and re-layouts  6.51 us
    all_to_all x1, starting transfers between devices, exchange(): lax.all_to_all(blocks, 'dev', split_axis=0, concat_axis=0, tiled=True)  5.8 us
    slice x3, local copies, waits for them, and re-layouts, attend(): key_value_cache[:, :, feature_width:]  4.05 us
    dot_general x3, matrix products, attend(): jnp.einsum('rsngc,rcnd->rsngd', probs_cache, cache_value_rows, preferred_...  3.54 us
  transfers between devices with their start and end apart: 5, of which 2 were waited for; matrix products, arithmetic and copies ran while one was open for 15% of the time, Pallas kernels for 1%

profile of v5, /device:TPU:1, one launch (start us, length us, event | category | flops | bytes accessed | tf_op | source)
XLA Modules:
  0.0 132.5 jit_solution(8427504892965827881)
XLA Ops:
  0.6 1.5 %collective-permute-start.1 = (bf16[32,4096]{1,0:T(8,128)(2,1)}, bf16[32,4096]{1,0:T(8,128)(2,1)S(1)}, u32[]{:S(2)}, u32[]{:S(2)}) collective-permute-start(bf16[32,4096]{1,0:T(8,128)(2,1)} %own_hbm.1), channel_id=1, source_target_pairs={{0,64},{64,0},{1,65},{65,1},{2,66},{66,2},{3,67},{67,3},{4,68},{68... | collective-permute-start | bytes 786440 | tf_op jit(solution)/shard_map/ppermute | solution.py:328
  2.2 0.4 collective-permute-start.2
  2.6 20.9 %conditional.2 = (bf16[32,8192]{1,0:T(8,128)(2,1)}) conditional(s32[]{:T(128)} %convert_element_type.102, () %tuple.28, (s32[8]{0:T(128)}, bf16[8,256,1024]{2,1,0:T(8,128)(2,1)}, bf16[32,8192]{1,0:T(8,128)(2,1)}, bf16[32,1024]{1,0:T(8,128)(2,1)}) %tuple.29), branch_computations={%region_0.0_spmd, %region_1.14_spmd} | conditional | flops 278984704 | bytes 55171180 | solution.py:331
  2.7 6.5 %copy.49 = bf16[8,256,1024]{1,2,0:T(8,128)(2,1)} copy(bf16[8,256,1024]{2,1,0:T(8,128)(2,1)} %get-tuple-element.80) | data formatting | bytes 8388608 | tf_op jit(solution)/shard_map
  9.2 2.1 %fusion.90 = (bf16[2,256,512]{1,2,0:T(8,128)(2,1)}, bf16[2,256,512]{1,2,0:T(8,128)(2,1)S(1)}) fusion(bf16[8,256,1024]{1,2,0:T(8,128)(2,1)} %copy.49), kind=kLoop, calls=%fused_computation.157 | loop fusion | bytes 2097152 | tf_op jit(solution)/shard_map/cond/branch_1_fun/slice | solution.py:33
  11.4 0.3 fusion.96
  11.8 0.4 fusion.97
  12.4 0.3 fusion.21
  12.9 1.4 %fusion.11 = bf16[2,4,4,16,128]{4,3,1,2,0:T(8,128)(2,1)S(1)} fusion(f32[2,4,4,16,128]{4,3,2,1,0:T(8,128)S(1)} %fusion.39, bf16[2,256,4,128,1]{1,3,4,2,0:T(8,128)(2,1)} %bitcast.279, f32[2,4,4,16,256]{4,3,1,2,0:T(8,128)S(1)} %get-tuple-element.100, f32[2,4,4,16]{3,1,2,0:T(4,128)S(1)} %add.62, f32[2,4,4,16]{3,1,2,0:T(4,128)S(1)} %max.42), kind=kOutput, calls=%fused_computation.17 | convolution fusion | flops 34078720 | bytes 1445888 | tf_op jit(solution)/shard_map/cond/branch_1_fun/rsngc,rcnd->rsngd/dot_general | solution.py:71
  14.4 0.9 fusion.92
  15.3 0.3 fusion.98
  15.7 0.4 fusion.99
  16.2 0.3 fusion.22
  16.5 0.2 fusion.40
  16.8 1.7 %fusion.10 = bf16[2,4,4,16,128]{4,3,1,2,0:T(8,128)(2,1)S(1)} fusion(f32[2,4,128,4,16]{2,4,3,1,0:T(8,128)S(1)} %fusion.40, bf16[2,256,4,128,1]{1,3,4,2,0:T(8,128)(2,1)} %bitcast.281, f32[2,4,4,16,256]{4,3,1,2,0:T(8,128)} %copy-done.5, f32[2,4,4,16]{3,1,2,0:T(4,128)S(1)} %add.64, f32[2,4,4,16]{3,1,2,0:T(4,128)S(1)} %max.43), kind=kOutput, calls=%fused_computation.16 | convolution fusion | flops 34078720 | bytes 1445888 | tf_op jit(solution)/shard_map/cond/branch_1_fun/rsngc,rcnd->rsngd/dot_general | solution.py:71
  18.7 1.1 fusion.91
  19.9 0.4 fusion.100
  20.4 0.8 fusion.101
  21.3 0.4 fusion.18
  21.7 0.3 fusion.34
  22.0 0.5 fusion.7
  22.7 0.8 pad_maximum_fusion
  23.5 0.4 find_spots.1.spots
  24.0 2.3 %place_rows.1 = bf16[512,4096]{1,0:T(8,128)(2,1)S(1)} custom-call(bf16[512,64]{1,0:T(8,128)(2,1)S(1)} %find_spots.1.spots, bf16[32,4096]{1,0:T(8,128)(2,1)} %own_hbm.1, bf16[32,4096]{1,0:T(8,128)(2,1)S(1)} %collective-permute-done.1.other_ref), custom_call_target="tpu_custom_call" | custom-call | tf_op jit(solution)/shard_map/place_rows/pallas_call | solution.py:155
  26.4 44.8 %all_to_all.10 = bf16[64,8,4096]{2,1,0:T(8,128)(2,1)S(1)} all-to-all(bf16[64,8,4096]{2,1,0:T(8,128)(2,1)S(1)} %bitcast.255), channel_id=1, replica_groups=mesh['role'=2,'dev'=64] {'dev'}, dimensions={0} | all-to-all | bytes 8388608 | tf_op jit(solution)/shard_map/all_to_all | solution.py:323
  71.2 11.0 %expert_layer.1 = bf16[512,4096]{1,0:T(8,128)(2,1)} custom-call(bf16[512,4096]{1,0:T(8,128)(2,1)S(1)} %bitcast.256, bf16[1,4096,1536]{2,1,0:T(8,128)(2,1)S(1)} %copy-done.2, bf16[1,768,4096]{2,1,0:T(8,128)(2,1)} %down_hbm.1), custom_call_target="tpu_custom_call" | custom-call | flops 9663676416 | bytes 8388608 | tf_op jit(solution)/shard_map/expert_layer/pallas_call | solution.py:273
  82.2 5.8 %all-to-all-start.1 = ((bf16[64,8,4096]{2,1,0:T(8,128)(2,1)}), bf16[64,8,4096]{2,1,0:T(8,128)(2,1)}, u32[]{:S(2)}, u32[]{:S(2)}) async-start(bf16[64,8,4096]{2,1,0:T(8,128)(2,1)} %bitcast.262), calls=%async_computation.1 | async-start | bytes 8388608 | tf_op jit(solution)/shard_map/all_to_all | solution.py:323
  88.1 0.6 weigh_lines.1.spread
  88.9 38.7 %all-to-all-done.1 = bf16[64,8,4096]{2,1,0:T(8,128)(2,1)} async-done(((bf16[64,8,4096]{2,1,0:T(8,128)(2,1)}), bf16[64,8,4096]{2,1,0:T(8,128)(2,1)}, u32[]{:S(2)}, u32[]{:S(2)}) %all-to-all-start.1) | async-done | bytes 4194336 | tf_op jit(solution)/shard_map/all_to_all | solution.py:323
  127.6 2.5 %mix_results.1 = (f32[32,4096]{1,0:T(8,128)S(1)}, bf16[32,4096]{1,0:T(8,128)(2,1)S(1)}) custom-call(bf16[128,512]{1,0:T(8,128)(2,1)S(1)} %weigh_lines.1.spread, bf16[512,4096]{1,0:T(8,128)(2,1)} %bitcast.84.in_hbm), custom_call_target="tpu_custom_call" | custom-call | tf_op jit(solution)/shard_map/mix_results/pallas_call | solution.py:221
  130.3 1.5 %collective-permute-done.3 = bf16[32,4096]{1,0:T(8,128)(2,1)S(1)} collective-permute-done((bf16[32,4096]{1,0:T(8,128)(2,1)S(1)}, bf16[32,4096]{1,0:T(8,128)(2,1)S(1)}, u32[]{:S(2)}, u32[]{:S(2)}) %collective-permute-start.3) | collective-permute-done | bytes 262176 | tf_op jit(solution)/shard_map/ppermute | solution.py:354
  131.8 0.7 add_convert_fusion
  (66 shorter events, 1.9 us)
Async XLA Ops:
  0.6 23.4 %collective-permute-start.1 = (bf16[32,4096]{1,0:T(8,128)(2,1)}, bf16[32,4096]{1,0:T(8,128)(2,1)S(1)}, u32[]{:S(2)}, u32[]{:S(2)}) collective-permute-start(bf16[32,4096]{1,0:T(8,128)(2,1)} %own_hbm.1), channel_id=1, source_target_pairs={{0,64},{64,0},{1,65},{65,1},{2,66},{66,2},{3,67},{67,3},{4,68},{68... | collective-permute-start | bytes 786440 | tf_op jit(solution)/shard_map/ppermute | solution.py:328
  2.1 21.4 %collective-permute-start = (s32[8,32]{1,0:T(8,128)}, s32[8,32]{1,0:T(8,128)S(1)}, u32[]{:S(2)}, u32[]{:S(2)}) collective-permute-start(s32[8,32]{1,0:T(8,128)} %bitcast.257), channel_id=1, source_target_pairs={{0,64},{64,0},{1,65},{65,1},{2,66},{66,2},{3,67},{67,3},{4,68},{68... | collective-permute-start | bytes 3080 | tf_op jit(solution)/shard_map/ppermute | solution.py:327
  2.2 21.8 %collective-permute-start.2 = (f32[8,32]{1,0:T(8,128)}, f32[8,32]{1,0:T(8,128)S(1)}, u32[]{:S(2)}, u32[]{:S(2)}) collective-permute-start(f32[8,32]{1,0:T(8,128)} %bitcast.260), channel_id=1, source_target_pairs={{0,64},{64,0},{1,65},{65,1},{2,66},{66,2},{3,67},{67,3},{4,68},{68... | collective-permute-start | bytes 3080 | tf_op jit(solution)/shard_map/ppermute | solution.py:329
  2.6 20.9 %copy-start = (s32[32,8]{0,1:T(8,128)S(1)}, s32[32,8]{0,1:T(8,128)}, u32[]{:S(2)}) copy-start(s32[32,8]{0,1:T(8,128)} %param.18) | copy-start | bytes 3076
  2.6 8.6 %copy-start.4 = (bf16[32,8192]{1,0:T(8,128)(2,1)S(1)}, bf16[32,8192]{1,0:T(8,128)(2,1)}, u32[]{:S(2)}) copy-start(bf16[32,8192]{1,0:T(8,128)(2,1)} %get-tuple-element.25) | copy-start | bytes 1572868 | tf_op jit(solution)/shard_map/cond
  2.6 8.6 %copy-start.9 = (s32[8]{0:T(128)S(1)}, s32[8]{0:T(128)}, u32[]{:S(2)}) copy-start(s32[8]{0:T(128)} %get-tuple-element.18) | copy-start | bytes 100 | tf_op jit(solution)/shard_map/cond
  2.6 9.1 %copy-start.7 = (bf16[32,1024]{1,0:T(8,128)(2,1)S(1)}, bf16[32,1024]{1,0:T(8,128)(2,1)}, u32[]{:S(2)}) copy-start(bf16[32,1024]{1,0:T(8,128)(2,1)} %get-tuple-element.26) | copy-start | bytes 196612 | tf_op jit(solution)/shard_map/cond
  11.3 3.1 %slice-start = ((bf16[8,256,1024]{1,2,0:T(8,128)(2,1)}), bf16[2,256,1024]{1,2,0:T(8,128)(2,1)S(1)}, s32[]{:S(2)}) async-start(bf16[8,256,1024]{1,2,0:T(8,128)(2,1)} %copy.49), calls=%async_computation.2 | async-start | bytes 2097152 | tf_op jit(solution)/shard_map/cond/branch_1_fun/split | solution.py:87
  11.8 3.9 %copy-start.10 = (pred[4,4]{1,0:T(4,128)(4,1)}, pred[4,4]{1,0:T(4,128)(4,1)S(1)}, u32[]{:S(2)}) copy-start(pred[4,4]{1,0:T(4,128)(4,1)S(1)} %iota_compare_fusion.2) | copy-start | bytes 52 | tf_op jit(solution)/shard_map/cond
  15.6 0.9 copy-start.5
  16.8 1.9 %slice-start.1 = ((bf16[8,256,1024]{1,2,0:T(8,128)(2,1)}), bf16[4,256,1024]{1,2,0:T(8,128)(2,1)S(1)}, s32[]{:S(2)}) async-start(bf16[8,256,1024]{1,2,0:T(8,128)(2,1)} %copy.49), calls=%async_computation.3 | async-start | bytes 4194304 | tf_op jit(solution)/shard_map/cond/branch_1_fun/split | solution.py:87
  18.6 1.8 %copy-start.11 = (pred[4,4]{1,0:T(4,128)(4,1)S(1)}, pred[4,4]{1,0:T(4,128)(4,1)}, u32[]{:S(2)}) copy-start(pred[4,4]{1,0:T(4,128)(4,1)} %copy-done.10) | copy-start | bytes 52 | tf_op jit(solution)/shard_map/cond
  19.9 2.2 %copy-start.6 = (bf16[4,256,512]{1,2,0:T(8,128)(2,1)S(1)}, bf16[4,256,512]{1,2,0:T(8,128)(2,1)}, u32[]{:S(2)}) copy-start(bf16[4,256,512]{1,2,0:T(8,128)(2,1)} %get-tuple-element.89) | copy-start | bytes 3145732 | tf_op jit(solution)/shard_map/cond
  24.0 47.2 %copy-start.2 = (bf16[1,4096,1536]{2,1,0:T(8,128)(2,1)S(1)}, bf16[1,4096,1536]{2,1,0:T(8,128)(2,1)}, u32[]{:S(2)}) copy-start(bf16[1,4096,1536]{2,1,0:T(8,128)(2,1)} %in_ref) | copy-start | bytes 37748740
  82.2 5.9 %copy-start.1 = (f32[32,8]{0,1:T(8,128)S(1)}, f32[32,8]{0,1:T(8,128)}, u32[]{:S(2)}) copy-start(f32[32,8]{0,1:T(8,128)} %param.19) | copy-start | bytes 3076
  82.2 6.5 %copy-start.3 = (bf16[32,8192]{1,0:T(8,128)(2,1)S(1)}, bf16[32,8192]{1,0:T(8,128)(2,1)}, u32[]{:S(2)}) copy-start(bf16[32,8192]{1,0:T(8,128)(2,1)} %param.13) | copy-start | bytes 1572868
  82.2 6.5 %copy-start.8 = (s32[8]{0:T(128)S(1)}, s32[8]{0:T(128)}, u32[]{:S(2)}) copy-start(s32[8]{0:T(128)} %param.16) | copy-start | bytes 100
  82.2 45.4 %all-to-all-start.1 = ((bf16[64,8,4096]{2,1,0:T(8,128)(2,1)}), bf16[64,8,4096]{2,1,0:T(8,128)(2,1)}, u32[]{:S(2)}, u32[]{:S(2)}) async-start(bf16[64,8,4096]{2,1,0:T(8,128)(2,1)} %bitcast.262), calls=%async_computation.1 | async-start | bytes 8388608 | tf_op jit(solution)/shard_map/all_to_all | solution.py:323
  130.2 1.6 %collective-permute-start.3 = (bf16[32,4096]{1,0:T(8,128)(2,1)S(1)}, bf16[32,4096]{1,0:T(8,128)(2,1)S(1)}, u32[]{:S(2)}, u32[]{:S(2)}) collective-permute-start(bf16[32,4096]{1,0:T(8,128)(2,1)S(1)} %get-tuple-element.78), channel_id=1, source_target_pairs={{0,64},{64,0},{1,65},{65,1},{2,66},{66,2},{3,67},{67,3},{4,68},{68... | collective-permute-start | bytes 786440 | tf_op jit(solution)/shard_map/ppermute | solution.py:354
